TPU v7x, 512 devices: a whole 4x8x8 slice. The times are simulated.
512 devices in a mesh: lat: 32 (over y_hi, z, core), lon: 16 (over y_lo, x).
Axes of the slice: x: 4, y: 8 (y_hi: 2, y_lo: 4; y = y_hi * 4 + y_lo), z: 8, core: 2. Of those that a mesh axis runs over, the one named last changes fastest.
Arguments:
- tokens: bfloat16 [128, 1024, 768], P('lat', 'lon'), may hold values from -6 to 6
- source_id: int32 [128, 1024], P('lat', 'lon'), may hold values from 0 to 4
- valid: int32 [128, 1024], P('lat', 'lon'), may hold values 0 or 1
- source_table: float32 [5, 768], replicated, may hold values from -3 to 3
- gain_lon: float32 [768], replicated, may hold values from 0.25 to 1.75
- gain_lat: float32 [768], replicated, may hold values from 0.25 to 1.75
- wqkv_lon: bfloat16 [768, 2304], P('lat', 'lon'), may hold values from -0.21650635 to 0.21650635
- wout_lon: bfloat16 [768, 768], P('lat', 'lon'), may hold values from -0.21875 to 0.21875
- wqkv_lat: bfloat16 [768, 2304], P('lat', 'lon'), may hold values from -0.21650635 to 0.21650635
- wout_lat: bfloat16 [768, 768], P('lat', 'lon'), may hold values from -0.21875 to 0.21875
Outputs:
- mixed: bfloat16 [128, 1024, 768], P('lat', 'lon')
All inputs are finite; a program needn't handle non-finite values. No bound on the sum of `valid` on one device may be relied on, other than what follows from the above.
Results may differ from a plain program's by a relative error of at most 0.0095.
Values may be sent and summed in bfloat16 or wider, within the bound.
A program may use at most 128 MiB of HBM per device.

v0:
```python
import jax
import jax.numpy as jnp
from jax import lax
from jax.sharding import PartitionSpec as P

HEADS = 16
HD = 48


def normalize(x, gain):
    scale = lax.rsqrt(jnp.mean(x * x, axis=-1, keepdims=True) + 1e-06)
    return (x * scale * gain).astype(jnp.bfloat16)


def fetch(weights):
    weights = (
        lax.all_gather(weights[0], "lon", axis=1, tiled=True),
        lax.all_gather(weights[1], "lon", axis=1, tiled=True),
    )
    weights = (
        lax.all_gather(weights[0], "lat", axis=0, tiled=True),
        lax.all_gather(weights[1], "lat", axis=0, tiled=True),
    )
    return weights


def attend(query, keys, values, keymask, form_scores, form_out):
    scale = 1.0 / jnp.sqrt(jnp.float32(query.shape[-1]))
    scores = jnp.einsum(form_scores, query, keys, preferred_element_type=jnp.float32) * scale
    scores = jnp.where(keymask > 0, scores, jnp.float32(-1e30))
    top = jnp.max(scores, axis=-1, keepdims=True)
    expo = jnp.exp(scores - top)
    probs = (expo / jnp.sum(expo, axis=-1, keepdims=True)).astype(jnp.bfloat16)
    return jnp.einsum(form_out, probs, values, preferred_element_type=jnp.float32).astype(
        jnp.bfloat16
    )


def project(normed, wqkv):
    lead = normed.shape[:-1]
    flat = normed.reshape(-1, normed.shape[-1])
    qkv = jnp.dot(flat, wqkv, preferred_element_type=jnp.float32).astype(jnp.bfloat16)
    qkv = qkv.reshape(lead + (3, HEADS, HD))
    return (qkv[..., 0, :, :], qkv[..., 1, :, :], qkv[..., 2, :, :])


def lat_attend(query, keys, values, keep):
    keymask = jnp.transpose(keep)[:, None, None, :]
    return attend(query, keys, values, keymask, "qbhd,kbhd->bhqk", "bhqk,kbhd->qbhd")


def local(
    tokens,
    source_id,
    valid,
    source_table,
    gain_lon,
    gain_lat,
    wqkv_lon,
    wout_lon,
    wqkv_lat,
    wout_lat,
):
    rows, cols, width = tokens.shape
    onehot = (source_id[:, :, None] == jnp.arange(source_table.shape[0], dtype=jnp.int32)).astype(
        jnp.float32
    )
    start = tokens.astype(jnp.float32) + jnp.einsum(
        "rcs,sd->rcd", onehot, source_table, precision=lax.Precision.HIGHEST
    )
    wqkv_one, wout_one = fetch((wqkv_lon, wout_lon))
    query, keys, values = project(normalize(start, gain_lon), wqkv_one)
    keep_heads = jnp.broadcast_to(valid[:, :, None], (rows, cols, HEADS))
    part_q = lax.all_to_all(query, "lon", split_axis=2, concat_axis=1, tiled=True)
    part_k = lax.all_to_all(keys, "lon", split_axis=2, concat_axis=1, tiled=True)
    part_v = lax.all_to_all(values, "lon", split_axis=2, concat_axis=1, tiled=True)
    part_m = lax.all_to_all(keep_heads, "lon", split_axis=2, concat_axis=1, tiled=True)
    keymask = jnp.transpose(part_m, (0, 2, 1))[:, :, None, :]
    row_out = attend(part_q, part_k, part_v, keymask, "bqhd,bkhd->bhqk", "bhqk,bkhd->bqhd")
    heads_out = lax.all_to_all(row_out, "lon", split_axis=1, concat_axis=2, tiled=True)
    middle = start + jnp.dot(
        heads_out.reshape(rows * cols, width), wout_one, preferred_element_type=jnp.float32
    ).reshape(rows, cols, width)
    wqkv_two, wout_two = fetch((wqkv_lat, wout_lat))
    normed = normalize(middle, gain_lat)
    query, keys, values = project(normed, wqkv_two)
    query, keys, values, keep_col = (
        lax.all_to_all(query, "lat", split_axis=1, concat_axis=0, tiled=True),
        lax.all_to_all(keys, "lat", split_axis=1, concat_axis=0, tiled=True),
        lax.all_to_all(values, "lat", split_axis=1, concat_axis=0, tiled=True),
        lax.all_to_all(valid, "lat", split_axis=1, concat_axis=0, tiled=True),
    )
    column_out = lat_attend(query, keys, values, keep_col)
    back = lax.all_to_all(column_out, "lat", split_axis=0, concat_axis=1, tiled=True)
    branch = jnp.dot(
        back.reshape(rows * cols, width), wout_two, preferred_element_type=jnp.float32
    ).reshape(rows, cols, width)
    return (middle + branch).astype(jnp.bfloat16)


def solution(mesh):
    placed = (
        P("lat", "lon", None),
        P("lat", "lon"),
        P("lat", "lon"),
        P(),
        P(),
        P(),
        P("lat", "lon"),
        P("lat", "lon"),
        P("lat", "lon"),
        P("lat", "lon"),
    )
    return jax.shard_map(
        local, mesh=mesh, in_specs=placed, out_specs=P("lat", "lon", None), check_vma=False
    )
```

profile of v0, /device:TPU:1, one launch (start us, length us, event | category | flops | bytes accessed | tf_op | source)
XLA Modules:
  0.0 551.0 jit_solution(10082784544614259530)
XLA Ops:
  6.6 37.7 %all-gather = bf16[16,144,24]{1,2,0:T(8,128)(2,1)S(1)} all-gather(bf16[1,144,24]{1,2,0:T(8,128)(2,1)} %bitcast.180), channel_id=1, replica_groups=mesh['lat'=32,'lon'=16] {'lon'}, dimensions={0}, use_global_device_ids=true | all-gather | bytes 117504 | tf_op jit(solution)/shard_map/all_gather | solution.py:17
  45.3 31.0 %all-gather.1 = bf16[16,48,24]{1,2,0:T(8,128)(2,1)S(1)} all-gather(bf16[1,48,24]{1,2,0:T(8,128)(2,1)} %bitcast.182), channel_id=1, replica_groups=mesh['lat'=32,'lon'=16] {'lon'}, dimensions={0}, use_global_device_ids=true | all-gather | bytes 39168 | tf_op jit(solution)/shard_map/all_gather | solution.py:18
  78.5 3.5 all-to-all-start.1
  82.0 38.9 %all-gather.2 = bf16[16,144,24]{1,2,0:T(8,128)(2,1)S(1)} all-gather(bf16[1,144,24]{1,2,0:T(8,128)(2,1)} %bitcast.181), channel_id=1, replica_groups=mesh['lat'=32,'lon'=16] {'lon'}, dimensions={0}, use_global_device_ids=true | all-gather | bytes 117504 | tf_op jit(solution)/shard_map/all_gather | solution.py:17
  122.7 30.9 %all-gather.9.cloned.1.call-done = bf16[768,2304]{1,0:T(8,128)(2,1)} async-done(((bf16[24,2304]{1,0:T(8,128)(2,1)}), bf16[768,2304]{1,0:T(8,128)(2,1)}) %all-gather.9.cloned.1.call-update) | async-done | bytes 3538960 | tf_op jit(solution)/shard_map/all_gather | solution.py:21
  153.6 3.1 convolution_convert_fusion.1
  156.7 1.4 copy.131
  158.1 3.6 reshape.99
  161.7 2.1 slice_bitcast_fusion.3
  163.9 3.0 reshape.116
  166.9 6.7 %all-to-all-start = ((bf16[16,2,6144]{2,1,0:T(2,128)(2,1)}), bf16[16,2,6144]{2,1,0:T(2,128)(2,1)S(1)}, u32[]{:S(2)}, u32[]{:S(2)}) async-start(bf16[16,2,6144]{2,1,0:T(2,128)(2,1)} %reshape.116), calls=%async_computation | async-start | bytes 786432 | tf_op jit(solution)/shard_map/all_to_all | solution.py:76
  174.9 10.7 %all-to-all-done = bf16[16,2,6144]{2,1,0:T(2,128)(2,1)S(1)} async-done(((bf16[16,2,6144]{2,1,0:T(2,128)(2,1)}), bf16[16,2,6144]{2,1,0:T(2,128)(2,1)S(1)}, u32[]{:S(2)}, u32[]{:S(2)}) %all-to-all-start) | async-done | bytes 393248 | tf_op jit(solution)/shard_map/all_to_all | solution.py:76
  185.6 4.5 all-to-all-start.2
  192.7 8.3 %all-to-all-done.2 = bf16[16,2,6144]{2,1,0:T(2,128)(2,1)S(1)} async-done(((bf16[16,2,6144]{2,1,0:T(2,128)(2,1)}), bf16[16,2,6144]{2,1,0:T(2,128)(2,1)S(1)}, u32[]{:S(2)}, u32[]{:S(2)}) %all-to-all-start.2) | async-done | bytes 393248 | tf_op jit(solution)/shard_map/all_to_all | solution.py:74
  201.0 5.6 %all-to-all-start.3 = ((bf16[16,2,6144]{2,1,0:T(2,128)(2,1)}), bf16[16,2,6144]{2,1,0:T(2,128)(2,1)S(1)}, u32[]{:S(2)}, u32[]{:S(2)}) async-start(bf16[16,2,6144]{2,1,0:T(2,128)(2,1)} %reshape.122), calls=%async_computation.3 | async-start | bytes 786432 | tf_op jit(solution)/shard_map/all_to_all | solution.py:75
  210.5 14.8 %all-to-all-done.3 = bf16[16,2,6144]{2,1,0:T(2,128)(2,1)S(1)} async-done(((bf16[16,2,6144]{2,1,0:T(2,128)(2,1)}), bf16[16,2,6144]{2,1,0:T(2,128)(2,1)S(1)}, u32[]{:S(2)}, u32[]{:S(2)}) %all-to-all-start.3) | async-done | bytes 393248 | tf_op jit(solution)/shard_map/all_to_all | solution.py:75
  227.2 8.9 %fusion.42 = (f32[4,1024]{1,0:T(4,128)S(1)}, f32[4,1024,1024]{1,2,0:T(8,128)}) fusion(pred[4,1024]{1,0:T(4,128)(4,1)S(1)} %gt.40, bf16[4,1024,48]{1,2,0:T(8,128)(2,1)S(1)} %reshape.101, bf16[4,1024,48]{1,2,0:T(8,128)(2,1)S(1)} %reshape.102), kind=kOutput, calls=%fused_computation.59 | convolution fusion | flops 419431424 | bytes 17584128 | tf_op jit(solution)/shard_map/sub | solution.py:32
  236.1 7.4 %fusion.13 = bf16[4,1024,1,48]{1,3,0,2:T(8,128)(2,1)S(1)} fusion(bf16[4,1024,48]{1,2,0:T(8,128)(2,1)S(1)} %reshape.100, f32[4,1024,1024]{1,2,0:T(8,128)} %get-tuple-element.14, f32[4,1024]{1,0:T(4,128)S(1)} %get-tuple-element.13), kind=kOutput, calls=%fused_computation.24 | convolution fusion | flops 411238400 | bytes 17580032 | tf_op jit(solution)/shard_map/bhqk,bkhd->bqhd/dot_general | solution.py:34
  244.2 2.4 reshape.124
  246.6 4.2 all-to-all-start.4
  251.5 11.1 %all-to-all-done.4 = bf16[16,2,6144]{2,1,0:T(2,128)(2,1)S(1)} async-done(((bf16[16,2,6144]{2,1,0:T(2,128)(2,1)}), bf16[16,2,6144]{2,1,0:T(2,128)(2,1)S(1)}, u32[]{:S(2)}, u32[]{:S(2)}) %all-to-all-start.4) | async-done | bytes 393248 | tf_op jit(solution)/shard_map/all_to_all | solution.py:80
  262.6 8.6 %all-to-all-start.6 = ((s32[4,32,2]{0,2,1:T(2,128)}), s32[4,32,2]{0,2,1:T(2,128)S(1)}, u32[]{:S(2)}, u32[]{:S(2)}) async-start(s32[4,32,2]{0,2,1:T(2,128)} %bitcast.33), calls=%async_computation.6 | async-start | bytes 65536 | tf_op jit(solution)/shard_map/all_to_all | solution.py:91
  274.2 1.9 multiply_reduce_fusion
  277.1 68.3 %all-gather.13.cloned.1.call-done = bf16[768,2304]{1,0:T(8,128)(2,1)} async-done(((bf16[24,2304]{1,0:T(8,128)(2,1)}), bf16[768,2304]{1,0:T(8,128)(2,1)}) %all-gather.13.cloned.1.call-update) | async-done | bytes 3538960 | tf_op jit(solution)/shard_map/all_gather | solution.py:21
  345.4 3.1 convolution_convert_fusion
  348.5 1.4 copy.141
  349.9 3.6 reshape.104
  353.6 2.4 slice_bitcast_fusion.1
  355.9 2.9 copy.142
  358.9 2.5 reshape.126
  361.3 4.2 all-to-all-start.5
  365.5 1.8 copy.150
  367.4 2.5 reshape.128
  369.8 10.5 %all-to-all-done.5 = bf16[32,2,3072]{2,1,0:T(2,128)(2,1)S(1)} async-done(((bf16[32,2,3072]{2,1,0:T(2,128)(2,1)}), bf16[32,2,3072]{2,1,0:T(2,128)(2,1)S(1)}, u32[]{:S(2)}, u32[]{:S(2)}) %all-to-all-start.5) | async-done | bytes 393248 | tf_op jit(solution)/shard_map/all_to_all | solution.py:90
  380.3 7.7 %all-to-all-start.8 = ((bf16[32,2,3072]{2,1,0:T(2,128)(2,1)}), bf16[32,2,3072]{2,1,0:T(2,128)(2,1)S(1)}, u32[]{:S(2)}, u32[]{:S(2)}) async-start(bf16[32,2,3072]{2,1,0:T(2,128)(2,1)} %reshape.128), calls=%async_computation.8 | async-start | bytes 786432 | tf_op jit(solution)/shard_map/all_to_all | solution.py:89
  388.0 1.8 copy.147
  389.8 2.5 reshape.130
  392.3 10.3 %all-to-all-done.8 = bf16[32,2,3072]{2,1,0:T(2,128)(2,1)S(1)} async-done(((bf16[32,2,3072]{2,1,0:T(2,128)(2,1)}), bf16[32,2,3072]{2,1,0:T(2,128)(2,1)S(1)}, u32[]{:S(2)}, u32[]{:S(2)}) %all-to-all-start.8) | async-done | bytes 393248 | tf_op jit(solution)/shard_map/all_to_all | solution.py:89
  402.6 7.7 %all-to-all-start.7 = ((bf16[32,2,3072]{2,1,0:T(2,128)(2,1)}), bf16[32,2,3072]{2,1,0:T(2,128)(2,1)}, u32[]{:S(2)}, u32[]{:S(2)}) async-start(bf16[32,2,3072]{2,1,0:T(2,128)(2,1)} %reshape.130), calls=%async_computation.7 | async-start | bytes 786432 | tf_op jit(solution)/shard_map/all_to_all | solution.py:88
  410.4 35.0 %all-gather.3 = bf16[16,48,24]{1,2,0:T(8,128)(2,1)S(1)} all-gather(bf16[1,48,24]{1,2,0:T(8,128)(2,1)S(1)} %bitcast.183), channel_id=1, replica_groups=mesh['lat'=32,'lon'=16] {'lon'}, dimensions={0}, use_global_device_ids=true | all-gather | bytes 39168 | tf_op jit(solution)/shard_map/all_gather | solution.py:18
  449.9 2.3 reshape.131
  453.7 2.1 fusion.17
  455.8 2.6 fusion.12
  458.4 1.5 copy.157
  459.8 1.7 reshape.132
  461.5 32.5 %all_to_all.151 = bf16[32,2,3072]{2,1,0:T(2,128)(2,1)S(1)} all-to-all(bf16[32,2,3072]{2,1,0:T(2,128)(2,1)S(1)} %reshape.132), channel_id=1, replica_groups=mesh['lat'=32,'lon'=16] {'lat'}, dimensions={0} | all-to-all | bytes 786432 | tf_op jit(solution)/shard_map/all_to_all | solution.py:94
  496.5 45.0 %all-gather.15.cloned.1.call-done = bf16[768,768]{1,0:T(8,128)(2,1)} async-done(((bf16[24,768]{1,0:T(8,128)(2,1)}), bf16[768,768]{1,0:T(8,128)(2,1)}) %all-gather.15.cloned.1.call-update) | async-done | bytes 1179664 | tf_op jit(solution)/shard_map/all_gather | solution.py:22
  541.5 2.5 fusion.10
  (92 shorter events, 28.4 us)
Async XLA Ops:
  6.5 115.4 %copy-start = (f32[5,768]{1,0:T(8,128)S(1)}, f32[5,768]{1,0:T(8,128)}, u32[]{:S(2)}) copy-start(f32[5,768]{1,0:T(8,128)} %param.13) | copy-start | bytes 46084
  6.5 115.4 %copy-start.13 = (s32[4,64]{1,0:T(4,128)S(1)}, s32[4,64]{1,0:T(4,128)}, u32[]{:S(2)}) copy-start(s32[4,64]{1,0:T(4,128)} %param.11) | copy-start | bytes 3076
  6.5 115.4 %copy-start.8 = (bf16[4,64,768]{2,1,0:T(8,128)(2,1)S(1)}, bf16[4,64,768]{2,1,0:T(8,128)(2,1)}, u32[]{:S(2)}) copy-start(bf16[4,64,768]{2,1,0:T(8,128)(2,1)} %param.10) | copy-start | bytes 1179652
  6.5 116.0 %copy-start.11 = (f32[768]{0:T(1024)S(1)}, f32[768]{0:T(1024)}, u32[]{:S(2)}) copy-start(f32[768]{0:T(1024)} %param.14) | copy-start | bytes 9220
  6.5 147.0 %all-gather.9.cloned.1.call-start = ((), (), s32[]{:S(2)}) async-start(), calls=%async_computation.10 | async-start | bytes 3649536 | tf_op jit(solution)/shard_map/all_gather | solution.py:21
  45.2 229.0 %all-gather.11.cloned.1.call-start = ((), (), s32[]{:S(2)}) async-start(), calls=%async_computation.11 | async-start | bytes 1216512 | tf_op jit(solution)/shard_map/all_gather | solution.py:22
  78.5 88.4 %all-to-all-start.1 = ((s32[16,1,256]{2,1,0:T(1,128)}), s32[16,1,256]{2,1,0:T(1,128)S(1)}, u32[]{:S(2)}, u32[]{:S(2)}) async-start(s32[16,1,256]{2,1,0:T(1,128)} %reshape.118), calls=%async_computation.1 | async-start | bytes 32768 | tf_op jit(solution)/shard_map/all_to_all | solution.py:77
  81.9 263.5 %all-gather.13.cloned.1.call-start = ((), (), s32[]{:S(2)}) async-start(), calls=%async_computation.12 | async-start | bytes 3649536 | tf_op jit(solution)/shard_map/all_gather | solution.py:21
  163.9 9.7 %copy-start.6 = (bf16[4,64,16,48]{1,0,3,2:T(4,128)(2,1)S(1)}, bf16[4,64,16,48]{1,0,3,2:T(4,128)(2,1)}, u32[]{:S(2)}) copy-start(bf16[4,64,16,48]{1,0,3,2:T(4,128)(2,1)} %get-tuple-element.9) | copy-start | bytes 1179652
  163.9 27.5 %copy-start.5 = (bf16[4,64,16,48]{1,0,3,2:T(4,128)(2,1)S(1)}, bf16[4,64,16,48]{1,0,3,2:T(4,128)(2,1)}, u32[]{:S(2)}) copy-start(bf16[4,64,16,48]{1,0,3,2:T(4,128)(2,1)} %get-tuple-element.8) | copy-start | bytes 1179652
  166.9 18.7 %all-to-all-start = ((bf16[16,2,6144]{2,1,0:T(2,128)(2,1)}), bf16[16,2,6144]{2,1,0:T(2,128)(2,1)S(1)}, u32[]{:S(2)}, u32[]{:S(2)}) async-start(bf16[16,2,6144]{2,1,0:T(2,128)(2,1)} %reshape.116), calls=%async_computation | async-start | bytes 786432 | tf_op jit(solution)/shard_map/all_to_all | solution.py:76
  185.6 15.4 %all-to-all-start.2 = ((bf16[16,2,6144]{2,1,0:T(2,128)(2,1)}), bf16[16,2,6144]{2,1,0:T(2,128)(2,1)S(1)}, u32[]{:S(2)}, u32[]{:S(2)}) async-start(bf16[16,2,6144]{2,1,0:T(2,128)(2,1)} %reshape.120), calls=%async_computation.2 | async-start | bytes 786432 | tf_op jit(solution)/shard_map/all_to_all | solution.py:74
  201.0 24.3 %all-to-all-start.3 = ((bf16[16,2,6144]{2,1,0:T(2,128)(2,1)}), bf16[16,2,6144]{2,1,0:T(2,128)(2,1)S(1)}, u32[]{:S(2)}, u32[]{:S(2)}) async-start(bf16[16,2,6144]{2,1,0:T(2,128)(2,1)} %reshape.122), calls=%async_computation.3 | async-start | bytes 786432 | tf_op jit(solution)/shard_map/all_to_all | solution.py:75
  243.5 7.3 %copy-start.9 = (s32[4,64]{1,0:T(4,128)S(1)}, s32[4,64]{1,0:T(4,128)}, u32[]{:S(2)}) copy-start(s32[4,64]{1,0:T(4,128)} %param.12) | copy-start | bytes 3076
  246.6 16.0 %all-to-all-start.4 = ((bf16[16,2,6144]{2,1,0:T(2,128)(2,1)}), bf16[16,2,6144]{2,1,0:T(2,128)(2,1)S(1)}, u32[]{:S(2)}, u32[]{:S(2)}) async-start(bf16[16,2,6144]{2,1,0:T(2,128)(2,1)} %reshape.124), calls=%async_computation.4 | async-start | bytes 786432 | tf_op jit(solution)/shard_map/all_to_all | solution.py:80
  262.6 98.7 %all-to-all-start.6 = ((s32[4,32,2]{0,2,1:T(2,128)}), s32[4,32,2]{0,2,1:T(2,128)S(1)}, u32[]{:S(2)}, u32[]{:S(2)}) async-start(s32[4,32,2]{0,2,1:T(2,128)} %bitcast.33), calls=%async_computation.6 | async-start | bytes 65536 | tf_op jit(solution)/shard_map/all_to_all | solution.py:91
  273.0 4.0 copy-start.12
  276.1 0.9 copy-start.2
  355.9 9.6 %copy-start.4 = (bf16[4,64,16,48]{1,0,3,2:T(4,128)(2,1)S(1)}, bf16[4,64,16,48]{1,0,3,2:T(4,128)(2,1)}, u32[]{:S(2)}) copy-start(bf16[4,64,16,48]{1,0,3,2:T(4,128)(2,1)} %get-tuple-element.6) | copy-start | bytes 1179652
  361.3 18.9 %all-to-all-start.5 = ((bf16[32,2,3072]{2,1,0:T(2,128)(2,1)}), bf16[32,2,3072]{2,1,0:T(2,128)(2,1)S(1)}, u32[]{:S(2)}, u32[]{:S(2)}) async-start(bf16[32,2,3072]{2,1,0:T(2,128)(2,1)} %reshape.126), calls=%async_computation.5 | async-start | bytes 786432 | tf_op jit(solution)/shard_map/all_to_all | solution.py:90
  380.3 22.4 %all-to-all-start.8 = ((bf16[32,2,3072]{2,1,0:T(2,128)(2,1)}), bf16[32,2,3072]{2,1,0:T(2,128)(2,1)S(1)}, u32[]{:S(2)}, u32[]{:S(2)}) async-start(bf16[32,2,3072]{2,1,0:T(2,128)(2,1)} %reshape.128), calls=%async_computation.8 | async-start | bytes 786432 | tf_op jit(solution)/shard_map/all_to_all | solution.py:89
  388.0 22.4 %copy-start.10 = (bf16[24,48]{1,0:T(8,128)(2,1)S(1)}, bf16[24,48]{1,0:T(8,128)(2,1)}, u32[]{:S(2)}) copy-start(bf16[24,48]{1,0:T(8,128)(2,1)} %param.19) | copy-start | bytes 6916
  402.6 47.2 %all-to-all-start.7 = ((bf16[32,2,3072]{2,1,0:T(2,128)(2,1)}), bf16[32,2,3072]{2,1,0:T(2,128)(2,1)}, u32[]{:S(2)}, u32[]{:S(2)}) async-start(bf16[32,2,3072]{2,1,0:T(2,128)(2,1)} %reshape.130), calls=%async_computation.7 | async-start | bytes 786432 | tf_op jit(solution)/shard_map/all_to_all | solution.py:88
  410.3 131.2 %all-gather.15.cloned.1.call-start = ((), (), s32[]{:S(2)}) async-start(), calls=%async_computation.13 | async-start | bytes 1216512 | tf_op jit(solution)/shard_map/all_gather | solution.py:22
  453.7 2.1 copy-start.7
  495.1 46.4 %copy-start.3 = (f32[4,64,768]{2,1,0:T(8,128)S(1)}, f32[4,64,768]{2,1,0:T(8,128)}, u32[]{:S(2)}) copy-start(f32[4,64,768]{2,1,0:T(8,128)} %copy-done.2) | copy-start | bytes 2359300
  495.1 48.9 %copy-start.1 = (f32[5,768]{1,0:T(8,128)S(1)}, f32[5,768]{1,0:T(8,128)}, u32[]{:S(2)}) copy-start(f32[5,768]{1,0:T(8,128)} %param.13) | copy-start | bytes 46084
Sparse Core Ops, SparseCore 0:
  45.4 108.1 all-gather.8
  156.8 84.0 all-gather.10
  244.2 101.1 all-gather.12
  446.3 95.1 all-gather.14
where the time goes:
time: 559 us; the launch traced here: 551 us
  waiting for transfers between devices  210 us (38%)
  blocking collectives  175 us (31%)
  local copies, waits for them, and re-layouts  64.5 us (12%)
  starting transfers between devices  52.8 us (9%)
  matrix products  33.4 us (6%)
  between operations  14.2 us (3%)
    all_gather x2, waiting for transfers between devices, fetch(): lax.all_gather(weights[0], 'lat', axis=0, tiled=True)  99.1 us
    all_gather x2, blocking collectives, fetch(): lax.all_gather(weights[0], 'lon', axis=1, tiled=True)  76.6 us
    all_gather x2, blocking collectives, fetch(): lax.all_gather(weights[1], 'lon', axis=1, tiled=True)  66 us
    all_gather x2, waiting for transfers between devices, fetch(): lax.all_gather(weights[1], 'lat', axis=0, tiled=True)  45 us
    all_to_all x1, blocking collectives, local(): lax.all_to_all(column_out, 'lat', split_axis=0, concat_axis=1, tiled=True)  32.5 us
    unnamed x52, local copies, waits for them, and re-layouts  31.5 us
    all_to_all x1, waiting for transfers between devices, local(): lax.all_to_all(keys, 'lon', split_axis=2, concat_axis=1, tiled=True)  14.8 us
  transfers between devices with their start and end apart: 13, of which 9 were waited for; matrix products, arithmetic and copies ran while one was open for 17% of the time, Pallas kernels for 0%

commit v1 on v0

v1 whole, which is shorter than its diff:
```python
import functools

import jax
import jax.numpy as jnp
from jax import lax
from jax.experimental import pallas as pl
from jax.experimental.pallas import tpu as pltpu
from jax.sharding import PartitionSpec as P

HEADS = 16
HD = 48
D = 768
NLAT = 32
NLON = 16
MESH = pl.DeviceIdType.MESH
BF = jnp.bfloat16
F32 = jnp.float32
ANY = pl.BlockSpec(memory_space=pl.ANY)
VMEM = pl.BlockSpec(memory_space=pltpu.VMEM)
DMA = pltpu.SemaphoreType.DMA
SCALE2 = float(1.4426950408889634 / (48.0**0.5))
LIMIT = 56 * 1024 * 1024


def normalize(x, gain):
    scale = lax.rsqrt(jnp.mean(x * x, axis=-1, keepdims=True) + 1e-06)
    return (x * scale * gain).astype(BF)


def where_am_i():
    return lax.axis_index("lat"), lax.axis_index("lon")


def remote(src, dst, send, recv, lat, lon):
    return pltpu.make_async_remote_copy(
        src_ref=src,
        dst_ref=dst,
        send_sem=send,
        recv_sem=recv,
        device_id=(lat, lon),
        device_id_type=MESH,
    )


def shifted(lat, lon, t, sign):
    core = lax.rem(lat, 2)
    dyi = t // 4
    off = dyi + 4 * (dyi // 3) + 4 * core * ((dyi // 2) * (3 - dyi))
    y = (lat // 16) * 4 + lon // 4
    y2 = lax.rem(y + off, 8) if sign > 0 else lax.rem(y + 8 - off, 8)
    dx = lax.rem(t, 4)
    x = lax.rem(lon, 4)
    x2 = lax.rem(x + dx, 4) if sign > 0 else lax.rem(x + 4 - dx, 4)
    return lax.rem(lat, 16) + 16 * (y2 // 4), lax.rem(y2, 4) * 4 + x2


def signal(sem, lat, lon):
    pl.semaphore_signal(sem, inc=1, device_id=(lat, lon), device_id_type=MESH)


def loop(lo, hi, body):
    def step(i, carry):
        body(i)
        return carry

    lax.fori_loop(lo, hi, step, 0)


def gather_lat_kernel(w_ref, v_ref, land, vlon, vlat, ws, wr, vls, vlr, vts, vtr):
    lat, lon = where_am_i()
    bar = pltpu.get_barrier_semaphore()
    loop(1, NLAT, lambda s: signal(bar, lax.rem(lat + s, NLAT), lon))
    loop(1, NLON, lambda s: signal(bar, lat, lax.rem(lon + s, NLON)))
    pl.semaphore_wait(bar, NLAT - 1 + NLON - 1)

    def wcopy(s):
        return remote(w_ref, land.at[lat], ws.at[s], wr.at[s], lax.rem(lat + s, NLAT), lon)

    def vtcopy(s):
        return remote(v_ref, vlat.at[lat], vts.at[s], vtr.at[s], lax.rem(lat + s, NLAT), lon)

    def vlcopy(s):
        return remote(v_ref, vlon.at[lon], vls.at[s], vlr.at[s], lat, lax.rem(lon + s, NLON))

    own = (
        pltpu.make_async_copy(w_ref, land.at[lat], wr.at[0]),
        pltpu.make_async_copy(v_ref, vlat.at[lat], vtr.at[0]),
        pltpu.make_async_copy(v_ref, vlon.at[lon], vlr.at[0]),
    )
    loop(1, NLAT, lambda s: wcopy(s).start())
    loop(1, NLON, lambda s: vlcopy(s).start())
    loop(1, NLAT, lambda s: vtcopy(s).start())
    for c in own:
        c.start()
    for c in own:
        c.wait()
    loop(1, NLAT, lambda s: wcopy(s).wait())
    loop(1, NLON, lambda s: vlcopy(s).wait())
    loop(1, NLAT, lambda s: vtcopy(s).wait())


def gather_lat(w, v):
    return pl.pallas_call(
        gather_lat_kernel,
        out_shape=(
            jax.ShapeDtypeStruct((NLAT, 24, 384), BF),
            jax.ShapeDtypeStruct((NLON, 8, 128), jnp.int32),
            jax.ShapeDtypeStruct((NLAT, 8, 128), jnp.int32),
        ),
        in_specs=[ANY, ANY],
        out_specs=(ANY, ANY, ANY),
        scratch_shapes=[DMA((NLAT,)), DMA((NLAT,)), DMA((NLON,)), DMA((NLON,)), DMA((NLAT,)), DMA((NLAT,))],
        compiler_params=pltpu.CompilerParams(collective_id=0, has_side_effects=True),
    )(w, v)


def head_unit(lon, i):
    u = lon * 3 + i
    return u // 16, lax.rem(u, 16)


def lon_in_kernel(x_ref, units, row, u1, ys, xs, rs, us, ur, own_sem):
    lat, lon = where_am_i()
    a, b = lon // 4, lax.rem(lon, 4)
    bar = pltpu.get_barrier_semaphore()

    def greet(t):
        p, q = shifted(lat, lon, t, 1)
        signal(bar, p, q)
        p, q = shifted(lat, lon, t, -1)
        signal(bar, p, q)

    loop(1, 16, greet)
    loop(1, 4, lambda s: signal(bar, lat, lax.rem(a + s, 4) * 4 + b))
    loop(1, 4, lambda s: signal(bar, lat, a * 4 + lax.rem(b + s, 4)))
    pl.semaphore_wait(bar, 36)

    def ycopy(s):
        to = lax.rem(a + s, 4)
        return remote(x_ref.at[to], row.at[b, a], ys.at[s], rs.at[b, a], lat, to * 4 + b)

    loop(1, 4, lambda s: ycopy(s).start())
    own = pltpu.make_async_copy(x_ref.at[a], row.at[b, a], own_sem)
    own.start()

    def each_unit(act):
        for i in range(3):
            part, h = head_unit(lon, i)
            slot = part * 4 + lax.rem(h, 4)
            g = h // 4

            def dest(dyi):
                t = dyi * 4 + lax.rem(g - b + 4, 4)
                p, q = shifted(lat, lon, t, 1)
                mine = t == 0
                far = remote(units.at[i], u1.at[slot], us.at[i, dyi], ur.at[slot], p, q)
                near = pltpu.make_async_copy(units.at[i], u1.at[slot], ur.at[slot])
                act(mine, far, near)

            loop(0, 4, dest)

    def begin(mine, far, near):
        @pl.when(mine)
        def _():
            near.start()

        @pl.when(jnp.logical_not(mine))
        def _():
            far.start()

    def finish(mine, far, near):
        @pl.when(jnp.logical_not(mine))
        def _():
            far.wait_send()

    each_unit(begin)
    own.wait()

    def xcopy(s, aa):
        to = lax.rem(b + s, 4)
        return remote(row.at[b, aa], row.at[b, aa], xs.at[s, aa], rs.at[b, aa], lat, a * 4 + to)

    def landed(bb, aa):
        return pltpu.make_async_copy(row.at[bb, aa], row.at[bb, aa], rs.at[bb, aa])

    loop(1, 4, lambda s: xcopy(s, a).start())

    def forward(s):
        src = lax.rem(a + 4 - s, 4)
        landed(b, src).wait()
        loop(1, 4, lambda k: xcopy(k, src).start())

    loop(1, 4, forward)

    def collect(s):
        src = lax.rem(b + s, 4)
        loop(0, 4, lambda aa: landed(src, aa).wait())

    loop(1, 4, collect)
    loop(0, 12, lambda k: pltpu.make_async_copy(u1.at[k], u1.at[k], ur.at[k]).wait())
    loop(1, 4, lambda s: ycopy(s).wait_send())
    loop(1, 4, lambda s: loop(0, 4, lambda aa: xcopy(s, aa).wait_send()))
    each_unit(finish)


def lon_in(x, units):
    return pl.pallas_call(
        lon_in_kernel,
        out_shape=(
            jax.ShapeDtypeStruct((4, 4, 64, D), BF),
            jax.ShapeDtypeStruct((12, HD, D), BF),
        ),
        in_specs=[ANY, ANY],
        out_specs=(ANY, ANY),
        scratch_shapes=[DMA((4,)), DMA((4, 4)), DMA((4, 4)), DMA((3, 4)), DMA((12,)), DMA],
        compiler_params=pltpu.CompilerParams(collective_id=1, has_side_effects=True),
    )(x, units)


def soft(k_aug, q_aug, v_aug):
    s = lax.dot_general(k_aug, q_aug, (((0,), (0,)), ((), ())), preferred_element_type=F32)
    m = jnp.max(s, axis=0, keepdims=True)
    p = jnp.exp2((s - m) * SCALE2).astype(BF)
    o = jnp.dot(v_aug, p, preferred_element_type=F32)
    return o[:HD] / o[HD : HD + 1]


def lon_attend_kernel(
    x_ref, w_ref, ka_ref, qa_ref, units, land, wo1, u2, wo2,
    q_s, kv_s, t_s, o_s, os, orr, s1, r1, s2, r2, s3, r3,
):
    lat, lon = where_am_i()
    a, b = lon // 4, lax.rem(lon, 4)
    core = lax.rem(lat, 2)
    bar = pltpu.get_barrier_semaphore()

    def greet(t):
        p, q = shifted(lat, lon, t, 1)
        signal(bar, p, q)
        p, q = shifted(lat, lon, t, -1)
        signal(bar, p, q)
        signal(bar, lat, lax.rem(lon + t, NLON))

    loop(1, 16, greet)
    pl.semaphore_wait(bar, 45)

    def wo1copy(t):
        p, q = shifted(lat, lon, t, 1)
        return remote(units.at[3], wo1.at[lon], s1.at[t], r1.at[lon], p, q)

    def wo2copy(t):
        p, q = shifted(lat, lon, t, 1)
        return remote(units.at[7], wo2.at[lon], s2.at[t], r2.at[lon], p, q)

    own1 = pltpu.make_async_copy(units.at[3], wo1.at[lon], r1.at[lon])
    own2 = pltpu.make_async_copy(units.at[7], wo2.at[lon], r2.at[lon])
    own1.start()
    own2.start()

    def u2do(act):
        for i in range(3):
            part, h = head_unit(lon, i)
            slot = part * 8 + lax.rem(h, 8)

            @pl.when(h // 8 == core)
            def _():
                def one(t):
                    p, q = shifted(lat, lon, t, 1)
                    c = remote(units.at[4 + i], u2.at[slot], s3.at[i, t], r3.at[slot], p, q)
                    if act == "start":
                        c.start()
                    else:
                        c.wait_send()

                loop(1, 16, one)
                if act == "start":
                    pltpu.make_async_copy(units.at[4 + i], u2.at[slot], r3.at[slot]).start()

    loop(1, 16, lambda t: wo1copy(t).start())
    u2do("start")
    loop(1, 16, lambda t: wo2copy(t).start())

    qkv = lax.dot_general(
        w_ref[...], x_ref[...], (((1,), (1,)), ((), ())), preferred_element_type=F32
    ).astype(BF)
    for h in range(4):
        for qb in range(4):
            q_s[qb, h] = qkv[h * HD : (h + 1) * HD, qb * 256 : (qb + 1) * 256]
        kv_s[h] = qkv[192 + h * HD : 192 + (h + 1) * HD]
        kv_s[4 + h] = qkv[384 + h * HD : 384 + (h + 1) * HD]
    o_s[...] = jnp.zeros_like(o_s)

    def ocopy(bb, aa):
        far = remote(o_s.at[bb, aa], land.at[lon], os.at[bb, aa], orr.at[lon], lat, aa * 4 + bb)
        near = pltpu.make_async_copy(o_s.at[bb, aa], land.at[lon], orr.at[lon])
        return aa * 4 + bb == lon, far, near

    def block(qb):
        def head(h):
            k_aug = jnp.concatenate([kv_s[h], ka_ref[...]], axis=0)
            q_aug = jnp.concatenate([q_s[qb, h], qa_ref[...]], axis=0)
            v_aug = jnp.concatenate([kv_s[4 + h], jnp.ones((16, 1024), BF)], axis=0)
            t_s[h] = soft(k_aug, q_aug, v_aug)

        loop(0, 4, head)
        o = jnp.transpose(t_s[...].reshape(192, 256)).astype(BF)
        for aa in range(4):
            o_s[qb, aa, :, :192] = o[aa * 64 : (aa + 1) * 64]

        def send(aa):
            mine, far, near = ocopy(qb, aa)

            @pl.when(mine)
            def _():
                near.start()

            @pl.when(jnp.logical_not(mine))
            def _():
                far.start()

        loop(0, 4, send)

    loop(0, 4, block)

    def done(qb):
        def one(aa):
            mine, far, near = ocopy(qb, aa)

            @pl.when(jnp.logical_not(mine))
            def _():
                far.wait_send()

        loop(0, 4, one)

    loop(0, 4, done)
    loop(0, 16, lambda k: pltpu.make_async_copy(land.at[k], land.at[k], orr.at[k]).wait())
    loop(0, 16, lambda k: pltpu.make_async_copy(wo1.at[k], wo1.at[k], r1.at[k]).wait())
    loop(0, 16, lambda k: pltpu.make_async_copy(wo2.at[k], wo2.at[k], r2.at[k]).wait())
    loop(0, 24, lambda k: pltpu.make_async_copy(u2.at[k], u2.at[k], r3.at[k]).wait())
    loop(1, 16, lambda t: wo1copy(t).wait_send())
    loop(1, 16, lambda t: wo2copy(t).wait_send())
    u2do("finish")


def lon_attend(x, w, ka, qa, units):
    return pl.pallas_call(
        lon_attend_kernel,
        out_shape=(
            jax.ShapeDtypeStruct((NLON, 64, 256), BF),
            jax.ShapeDtypeStruct((16, HD, D), BF),
            jax.ShapeDtypeStruct((24, HD, D), BF),
            jax.ShapeDtypeStruct((16, HD, D), BF),
        ),
        in_specs=[VMEM, VMEM, VMEM, VMEM, ANY],
        out_specs=(ANY, ANY, ANY, ANY),
        scratch_shapes=[
            pltpu.VMEM((4, 4, HD, 256), BF),
            pltpu.VMEM((8, HD, 1024), BF),
            pltpu.VMEM((4, HD, 256), F32),
            pltpu.VMEM((4, 4, 64, 256), BF),
            DMA((4, 4)), DMA((16,)), DMA((16,)), DMA((16,)), DMA((16,)), DMA((16,)), DMA((3, 16)), DMA((24,)),
        ],
        compiler_params=pltpu.CompilerParams(
            collective_id=2, has_side_effects=True, vmem_limit_bytes=LIMIT
        ),
    )(x, w, ka, qa, units)


def lat_attend_kernel(x_ref, w_ref, ka_ref, qa_ref, back, col, qkv_s, t_s, o_s, xs, xr, bs, br):
    lat, lon = where_am_i()
    bar = pltpu.get_barrier_semaphore()
    loop(1, NLAT, lambda s: signal(bar, lax.rem(lat + s, NLAT), lon))
    pl.semaphore_wait(bar, NLAT - 1)

    def xcopy(s):
        to = lax.rem(lat + s, NLAT)
        return remote(x_ref.at[to // 2], col.at[lat], xs.at[s], xr.at[s], to, lon)

    def bcopy(s):
        to = lax.rem(lat + s, NLAT)
        return remote(o_s.at[to], back.at[lat], bs.at[s], br.at[s], to, lon)

    loop(1, NLAT, lambda s: xcopy(s).start())
    own = pltpu.make_async_copy(x_ref.at[lat // 2], col.at[lat], xr.at[0])
    own.start()
    own.wait()
    loop(1, NLAT, lambda s: xcopy(s).wait())
    x = col[...].reshape(512, D)
    qkv = lax.dot_general(
        w_ref[...], x, (((1,), (1,)), ((), ())), preferred_element_type=F32
    ).astype(BF)
    qkv_s[...] = qkv.reshape(24, HD, 512)

    def head(h):
        k_aug = jnp.concatenate([qkv_s[8 + h], ka_ref[...]], axis=0)
        q_aug = jnp.concatenate([qkv_s[h], qa_ref[...]], axis=0)
        v_aug = jnp.concatenate([qkv_s[16 + h], jnp.ones((16, 512), BF)], axis=0)
        t_s[h] = soft(k_aug, q_aug, v_aug)

    loop(0, 8, head)
    o = jnp.transpose(t_s[...].reshape(384, 512)).astype(BF)
    o_s[...] = o.reshape(NLAT, 16, 384)
    loop(1, NLAT, lambda s: bcopy(s).start())
    mine = pltpu.make_async_copy(o_s.at[lat], back.at[lat], br.at[0])
    mine.start()
    mine.wait()
    loop(1, NLAT, lambda s: bcopy(s).wait())


def lat_attend(x, w, ka, qa):
    return pl.pallas_call(
        lat_attend_kernel,
        out_shape=jax.ShapeDtypeStruct((NLAT, 16, 384), BF),
        in_specs=[VMEM, VMEM, VMEM, VMEM],
        out_specs=ANY,
        scratch_shapes=[
            pltpu.VMEM((NLAT, 16, D), BF),
            pltpu.VMEM((24, HD, 512), BF),
            pltpu.VMEM((8, HD, 512), F32),
            pltpu.VMEM((NLAT, 16, 384), BF),
            DMA((NLAT,)), DMA((NLAT,)), DMA((NLAT,)), DMA((NLAT,)),
        ],
        compiler_params=pltpu.CompilerParams(
            collective_id=3, has_side_effects=True, vmem_limit_bytes=LIMIT
        ),
    )(x, w, ka, qa)


def local(
    tokens, source_id, valid, source_table, gain_lon, gain_lat, wqkv_lon, wout_lon, wqkv_lat, wout_lat
):
    rows, cols, width = tokens.shape
    onehot = (source_id[:, :, None] == jnp.arange(source_table.shape[0], dtype=jnp.int32)).astype(F32)
    start = tokens.astype(F32) + jnp.einsum(
        "rcs,sd->rcd", onehot, source_table, precision=lax.Precision.HIGHEST
    )
    lat, lon = where_am_i()
    shard = jnp.concatenate([wqkv_lon, wout_lon, wqkv_lat, wout_lat], axis=1)
    land, vlon, vlat = gather_lat(shard, jnp.pad(valid, ((0, 4), (0, 64))))
    units = land.reshape(D, 384).T.reshape(8, HD, D)
    keep = lax.dynamic_index_in_dim(vlon, lon // 4, 1, keepdims=False)[:, :64]
    keep = keep.reshape(4, 4, 64).transpose(1, 0, 2).reshape(1, 1024)
    ka1 = jnp.pad(jnp.where(keep > 0, 0.0, -1e30).astype(BF), ((0, 15), (0, 0)))
    qa1 = jnp.pad(jnp.ones((1, 1024), BF), ((0, 15), (0, 0)))[:, :256]

    xn = normalize(start, gain_lon)
    row, u1 = lon_in(xn, units)
    land1, wo1, u2, wo2 = lon_attend(row.reshape(1024, D), u1.reshape(576, D), ka1, qa1, units)
    heads = land1.reshape(4, 4, 64, 256)[..., :192].transpose(0, 2, 1, 3).reshape(rows * cols, width)
    middle = start + lax.dot_general(
        heads, wo1.reshape(D, D), (((1,), (1,)), ((), ())), preferred_element_type=F32
    ).reshape(rows, cols, width)

    xn2 = normalize(middle, gain_lat).reshape(4, 16, 4, D).transpose(1, 0, 2, 3).reshape(16, 16, D)
    keep2 = lax.dynamic_slice_in_dim(vlat[:, :4, :], (lat // 2) * 4, 4, 2).reshape(1, 512)
    column = lax.broadcasted_iota(jnp.int32, (4, 512), 1) % 4
    same = column == lax.broadcasted_iota(jnp.int32, (4, 512), 0)
    ka2 = jnp.concatenate(
        [jnp.where(keep2 > 0, 0.0, -1e30), same.astype(F32), jnp.zeros((11, 512), F32)], axis=0
    ).astype(BF)
    qa2 = jnp.concatenate(
        [jnp.ones((1, 512), F32), jnp.where(same, 0.0, -1e34), jnp.zeros((11, 512), F32)], axis=0
    ).astype(BF)
    back = lat_attend(xn2, u2.reshape(1152, D), ka2, qa2)
    heads2 = back.reshape(16, 2, 4, 4, 384).transpose(2, 0, 3, 1, 4).reshape(rows * cols, width)
    branch = lax.dot_general(
        heads2, wo2.reshape(D, D), (((1,), (1,)), ((), ())), preferred_element_type=F32
    ).reshape(rows, cols, width)
    return (middle + branch).astype(BF)


def solution(mesh):
    placed = (
        P("lat", "lon", None),
        P("lat", "lon"),
        P("lat", "lon"),
        P(),
        P(),
        P(),
        P("lat", "lon"),
        P("lat", "lon"),
        P("lat", "lon"),
        P("lat", "lon"),
    )
    return jax.shard_map(
        local, mesh=mesh, in_specs=placed, out_specs=P("lat", "lon", None), check_vma=False
    )
```

time: 559 us -> 228 us (0.41); the launches traced: 551 us -> 226 us
  waiting for transfers between devices: 210 us -> 0 us
  Pallas kernels: 0 us -> 209 us
  blocking collectives: 175 us -> 0 us
  local copies, waits for them, and re-layouts: 64.5 us -> 11.2 us
  starting transfers between devices: 52.8 us -> 0 us
  matrix products: 33.4 us -> 2.5 us
  between operations: 14.2 us -> 0.26 us
    pallas_call x0 -> x4, Pallas kernels: none -> 209 us  [the longest x1 74.3 us: lon_attend(): pl.pallas_call(lon_attend_kernel, out_shape=(jax.ShapeDtypeStruct((NLON,...]
    all_gather x4 -> x0, waiting for transfers between devices: 144 us -> none  [the longest x2 99.1 us: fetch(): lax.all_gather(weights[0], 'lat', axis=0, tiled=True)]
    all_gather x4 -> x0, blocking collectives: 143 us -> none  [the longest x2 76.6 us: fetch(): lax.all_gather(weights[0], 'lon', axis=1, tiled=True)]
    all_to_all x9 -> x0, waiting for transfers between devices: 65.7 us -> none  [the longest x1 14.8 us: local(): lax.all_to_all(keys, 'lon', split_axis=2, concat_axis=1, tiled=True)]
    all_to_all x9 -> x0, starting transfers between devices: 52.7 us -> none  [the longest x1 8.63 us: local(): lax.all_to_all(valid, 'lat', split_axis=1, concat_axis=0, tiled=True)]
    all_to_all x1 -> x0, blocking collectives: 32.5 us -> none  [local(): lax.all_to_all(column_out, 'lat', split_axis=0, concat_axis=1, tiled=True)]
    unnamed x52 -> x18, local copies, waits for them, and re-layouts: 31.5 us -> 0.49 us
    dot_general x7 -> x2, matrix products: 22.6 us -> 1.86 us  [the longest x1 1.26 us: local(): lax.dot_general(heads2, wo2.reshape(D, D), (((1,), (1,)), ((), ())), pref...]
  transfers between devices with their start and end apart: 13 -> 0, of which waited for: 9 -> 0; matrix products, arithmetic and copies ran while one was open for 17% -> 0% of each run, Pallas kernels for 0% -> 0%
where the time goes in v1:
time: 228 us; the launch traced here: 226 us
  Pallas kernels  209 us (92%)
  local copies, waits for them, and re-layouts  11.2 us (5%)
  other arithmetic  3.3 us (1%)
  matrix products  2.5 us (1%)
    pallas_call x1, Pallas kernels, lon_attend(): pl.pallas_call(lon_attend_kernel, out_shape=(jax.ShapeDtypeStruct((NLON,...  74.3 us
    pallas_call x1, Pallas kernels, lat_attend(): pl.pallas_call(lat_attend_kernel, out_shape=jax.ShapeDtypeStruct((NLAT, 1...  55.8 us
    pallas_call x1, Pallas kernels, lon_in(): pl.pallas_call(lon_in_kernel, out_shape=(jax.ShapeDtypeStruct((4, 4, 64,...  39.6 us
    pallas_call x1, Pallas kernels, gather_lat(): pl.pallas_call(gather_lat_kernel, out_shape=(jax.ShapeDtypeStruct((NLAT,...  39.2 us

profile of v1, /device:TPU:1, one launch (start us, length us, event | category | flops | bytes accessed | tf_op | source)
XLA Modules:
  0.0 226.2 jit_solution(2845940051480269683)
XLA Ops:
  0.0 0.0 copy-start
  0.0 0.0 copy-start.7
  0.0 0.0 copy-start.3
  0.1 0.1 pad.16.clone
  0.1 1.3 pad.9.v_ref
  1.5 1.4 pad_maximum_fusion.w_ref
  2.9 39.2 %shard_map.100 = (bf16[32,24,384]{2,1,0:T(8,128)(2,1)}, s32[16,8,128]{2,1,0:T(8,128)}, s32[32,8,128]{2,1,0:T(8,128)}) custom-call(bf16[24,384]{1,0:T(8,128)(2,1)} %pad_maximum_fusion.w_ref, s32[8,128]{1,0:T(8,128)} %pad.9.v_ref), custom_call_target="tpu_custom_call" | custom-call | tf_op jit(solution)/shard_map/pallas_call | solution.py:103
  42.1 0.0 copy-start.4
  42.1 0.0 copy-start.5
  42.1 2.2 copy.15
  44.3 0.8 constant_dynamic-slice_fusion
  45.2 0.1 convert_element_type.39
  45.3 0.6 pad.10.ka_ref
  45.9 0.0 copy-done.4
  45.9 0.1 select_convert_fusion
  46.0 0.1 select_n.66
  46.1 0.7 maximum_maximum_fusion.1
  46.8 0.0 copy-done
  46.8 0.0 copy-done.7
  46.8 0.0 copy-done.3
  46.8 0.6 multiply_reduce_fusion.1
  47.5 0.0 copy-start.8
  47.5 0.0 copy-done.5
  47.5 0.9 multiply_convert_fusion.1.x_ref
  48.4 39.6 %shard_map.101 = (bf16[4,4,64,768]{3,2,1,0:T(8,128)(2,1)}, bf16[12,48,768]{2,1,0:T(8,128)(2,1)}) custom-call(bf16[4,64,768]{2,1,0:T(8,128)(2,1)} %multiply_convert_fusion.1.x_ref, bf16[8,48,768]{2,1,0:T(8,128)(2,1)} %bitcast.34), custom_call_target="tpu_custom_call" | custom-call | tf_op jit(solution)/shard_map/pallas_call | solution.py:207
  88.0 0.0 copy-done.8
  88.0 0.7 slice.13.qa_ref
  88.7 74.3 %shard_map.102 = (bf16[16,64,256]{2,1,0:T(8,128)(2,1)}, bf16[16,48,768]{2,1,0:T(8,128)(2,1)}, bf16[24,48,768]{2,1,0:T(8,128)(2,1)}, bf16[16,48,768]{2,1,0:T(8,128)(2,1)}) custom-call(bf16[1024,768]{1,0:T(8,128)(2,1)} %bitcast.37, bf16[576,768]{1,0:T(8,128)(2,1)} %bitcast.42, bf16[16,1024]{1,0:T(8,128)(2,1)} %pad.10.ka_ref, bf16[16,256]{1,0:T(8,128)(2,1)} %slice.13.qa_ref, ...), custom_call_target="tpu_custom_call" | custom-call | tf_op jit(solution)/shard_map/pallas_call | solution.py:346
  163.0 1.1 slice_bitcast_fusion
  164.1 0.0 copy-start.2
  164.1 0.4 copy.17
  164.5 0.5 dot_general.14
  165.0 0.4 copy-done.2
  165.4 0.0 copy-start.6
  165.4 0.6 multiply_reduce_fusion
  166.0 0.1 copy-done.6
  166.1 0.1 multiply_convert_fusion
  166.2 0.1 reshape.124
  166.3 0.1 copy.21
  166.4 0.8 reshape.125.x_ref
  167.3 55.8 %shard_map.103 = bf16[32,16,384]{2,1,0:T(8,128)(2,1)} custom-call(bf16[16,16,768]{2,1,0:T(8,128)(2,1)} %reshape.125.x_ref, bf16[1152,768]{1,0:T(8,128)(2,1)} %bitcast.36, bf16[16,512]{1,0:T(8,128)(2,1)} %get-tuple-element.24.ka_ref, bf16[16,512]{1,0:T(8,128)(2,1)} %get-tuple-element.23.qa_ref), custom_call_target="tpu_custom_call" | custom-call | tf_op jit(solution)/shard_map/pallas_call | solution.py:411
  223.1 0.0 copy-start.1
  223.1 1.2 reshape.127
  224.3 0.3 copy.19
  224.6 0.2 dot_general.16
  224.9 0.0 copy-done.1
  224.9 1.3 fusion
  (11 shorter events, 0.1 us)
Async XLA Ops:
  0.0 46.8 %copy-start = (f32[5,768]{1,0:T(8,128)S(1)}, f32[5,768]{1,0:T(8,128)}, u32[]{:S(2)}) copy-start(f32[5,768]{1,0:T(8,128)} %param.13) | copy-start | bytes 46084
  0.0 46.8 %copy-start.7 = (s32[4,64]{1,0:T(4,128)S(1)}, s32[4,64]{1,0:T(4,128)}, u32[]{:S(2)}) copy-start(s32[4,64]{1,0:T(4,128)} %param.11) | copy-start | bytes 3076
  0.0 46.8 %copy-start.3 = (bf16[4,64,768]{2,1,0:T(8,128)(2,1)S(1)}, bf16[4,64,768]{2,1,0:T(8,128)(2,1)}, u32[]{:S(2)}) copy-start(bf16[4,64,768]{2,1,0:T(8,128)(2,1)} %param.10) | copy-start | bytes 1179652
  42.1 3.8 %copy-start.4 = (s32[32,8,128]{2,1,0:T(8,128)S(1)}, s32[32,8,128]{2,1,0:T(8,128)}, u32[]{:S(2)}) copy-start(s32[32,8,128]{2,1,0:T(8,128)} %get-tuple-element.21) | copy-start | bytes 393220
  42.1 5.4 %copy-start.5 = (f32[768]{0:T(1024)S(1)}, f32[768]{0:T(1024)}, u32[]{:S(2)}) copy-start(f32[768]{0:T(1024)} %param.14) | copy-start | bytes 9220
  47.5 40.5 %copy-start.8 = (bf16[16]{0:T(256)(128)(2,1)S(1)}, bf16[16]{0:T(256)(128)(2,1)}, u32[]{:S(2)}) copy-start(bf16[16]{0:T(256)(128)(2,1)} %constant.73.clone.1) | copy-start | bytes 100
  164.1 1.3 copy-start.2
  165.4 0.7 copy-start.6
  223.1 1.8 copy-start.1

commit v2 on v0

v2 whole, which is shorter than its diff:
```python
import functools

import jax
import jax.numpy as jnp
from jax import lax
from jax.experimental import pallas as pl
from jax.experimental.pallas import tpu as pltpu
from jax.sharding import PartitionSpec as P

HEADS = 16
HD = 48
D = 768
NLAT = 32
NLON = 16
MESH = pl.DeviceIdType.MESH
BF = jnp.bfloat16
F32 = jnp.float32
VMEM = pl.BlockSpec(memory_space=pltpu.VMEM)
DMA = pltpu.SemaphoreType.DMA
SCALE2 = float(1.4426950408889634 / (48.0**0.5))
LIMIT = 56 * 1024 * 1024


def normalize(x, gain):
    scale = lax.rsqrt(jnp.mean(x * x, axis=-1, keepdims=True) + 1e-06)
    return (x * scale * gain).astype(BF)


def nt(x, y):
    return lax.dot_general(x, y, (((1,), (1,)), ((), ())), preferred_element_type=F32)


def where_am_i():
    return lax.axis_index("lat"), lax.axis_index("lon")


def remote(src, dst, send, recv, lat, lon):
    return pltpu.make_async_remote_copy(
        src_ref=src,
        dst_ref=dst,
        send_sem=send,
        recv_sem=recv,
        device_id=(lat, lon),
        device_id_type=MESH,
    )


def shifted(lat, lon, t, sign):
    core = lax.rem(lat, 2)
    dyi = t // 4
    off = dyi + 4 * (dyi // 3) + 4 * core * ((dyi // 2) * (3 - dyi))
    y = (lat // 16) * 4 + lon // 4
    y2 = lax.rem(y + off, 8) if sign > 0 else lax.rem(y + 8 - off, 8)
    dx = lax.rem(t, 4)
    x = lax.rem(lon, 4)
    x2 = lax.rem(x + dx, 4) if sign > 0 else lax.rem(x + 4 - dx, 4)
    return lax.rem(lat, 16) + 16 * (y2 // 4), lax.rem(y2, 4) * 4 + x2


def signal(sem, lat, lon):
    pl.semaphore_signal(sem, inc=1, device_id=(lat, lon), device_id_type=MESH)


def loop(lo, hi, body):
    def step(i, carry):
        body(i)
        return carry

    lax.fori_loop(lo, hi, step, 0)


def head_unit(lon, i):
    u = lon * 3 + i
    return u // 16, lax.rem(u, 16)


def soft(k_aug, q_aug, v_aug):
    s = lax.dot_general(k_aug, q_aug, (((0,), (0,)), ((), ())), preferred_element_type=F32)
    m = jnp.max(s, axis=0, keepdims=True)
    p = jnp.exp2((s - m) * SCALE2).astype(BF)
    o = jnp.dot(v_aug, p, preferred_element_type=F32)
    return o[:HD] / o[HD : HD + 1]


def arrived(ref, sem):
    return pltpu.make_async_copy(ref, ref, sem)


def pair_kernel(
    shard, tok, sid, table, g1, g2, v1, v2, e_ref, qa1, ka2c, qa2, out,
    land, units, start_s, xn_s, row, u1, wo1, u2, wo2, vl, mv, q_s, kv_s, t_s, o_s, land_o,
    x2_s, col, qkv2, t2, o2_s, back,
    s1s, s1r, sbs, sbr, v1s, v1r, v2s, v2r, ys, xs, rr, u1s, u1r, u1f, w1s, w1r, w1f, u2s, u2r,
    w2s, w2r, w2f, os, orr, x2s, x2r, x2f, bs, br,
):
    lat, lon = where_am_i()
    a, b = lon // 4, lax.rem(lon, 4)
    core, place = lax.rem(lat, 2), lat // 2
    sib = lat + 1 - 2 * core

    bar = pltpu.get_barrier_semaphore()
    loop(1, NLAT, lambda s: signal(bar, lax.rem(lat + s, NLAT), lon))

    def greet(t):
        p, q = shifted(lat, lon, t, -1)
        signal(bar, p, q)
        signal(bar, lat, lax.rem(lon + t, NLON))

    loop(1, 16, greet)
    pl.semaphore_wait(bar, 61)

    def wcopy(s):
        to = lax.rem(place + s, 16)
        return remote(shard, land.at[core, place], s1s.at[s], s1r.at[place], to * 2 + core, lon)

    loop(1, 16, lambda s: wcopy(s).start())
    land[core, place] = shard[...]

    kind = lax.broadcasted_iota(jnp.int32, (8, 256), 0)
    onehot = jnp.where(kind == sid[...], 1.0, 0.0)
    emb = lax.dot_general(
        onehot, table[...], (((0,), (0,)), ((), ())),
        precision=lax.Precision.HIGHEST, preferred_element_type=F32,
    )
    start = tok[...].astype(F32) + emb
    start_s[...] = start
    xn_s[...] = normalize(start, g1[...]).reshape(4, 64, D)

    def ycopy(s):
        to = lax.rem(a + s, 4)
        return remote(xn_s.at[to], row.at[b, a], ys.at[s], rr.at[b, a], lat, to * 4 + b)

    def xcopy(s, aa):
        to = lax.rem(b + s, 4)
        return remote(row.at[b, aa], row.at[b, aa], xs.at[s, aa], rr.at[b, aa], lat, a * 4 + to)

    loop(1, 4, lambda s: ycopy(s).start())
    row[b, a] = xn_s[a]
    loop(1, 4, lambda s: xcopy(s, a).start())

    def v1copy(s):
        to = lax.rem(lon + s, NLON)
        return remote(v1.at[to // 4], vl.at[lon], v1s.at[s], v1r.at[lon], lat, to)

    def v2copy(s):
        to = lax.rem(lat + s, NLAT)
        return remote(v2.at[to // 2], mv.at[core, place], v2s.at[s], v2r.at[core, place], to, lon)

    loop(1, 16, lambda s: v1copy(s).start())
    loop(1, NLAT, lambda s: v2copy(s).start())
    vl[lon] = v1[a]
    mv[core, place] = v2[place]

    def missing(s):
        src = lax.rem(place + 16 - s, 16)
        arrived(land.at[core, src], s1r.at[src]).wait()

    loop(1, 16, missing)
    sibling = remote(land.at[core], land.at[core], sbs, sbr, sib, lon)
    sibling.start()

    def forward(s):
        src = lax.rem(a + 4 - s, 4)
        arrived(row.at[b, src], rr.at[b, src]).wait()
        loop(1, 4, lambda k: xcopy(k, src).start())

    loop(1, 4, forward)
    arrived(land.at[1 - core], sbr).wait()

    w = land[...].astype(F32)
    w = jnp.stack([w[0], w[1]], axis=1).reshape(D, 384)
    units[...] = jnp.transpose(w).astype(BF).reshape(8, HD, D)

    def each_u1(act):
        for i in range(3):
            part, h = head_unit(lon, i)
            slot = part * 4 + lax.rem(h, 4)
            g = h // 4

            @pl.when(lax.rem(h, 2) == core)
            def _():
                def dest(dyi):
                    t = dyi * 4 + lax.rem(g - b + 4, 4)
                    p, q = shifted(lat, lon, t, 1)
                    far = remote(units.at[i], u1.at[slot], u1s.at[i, dyi], u1r.at[slot], p, q)

                    @pl.when(t == 0)
                    def _():
                        if act == "start":
                            pltpu.make_async_copy(units.at[i], u1.at[slot], u1r.at[slot]).start()

                    @pl.when(t != 0)
                    def _():
                        if act == "start":
                            far.start()
                        else:
                            far.wait_send()

                loop(0, 4, dest)

    each_u1("start")

    def wcast(unit, dst, ssem, rsem):
        def one(t):
            p, q = shifted(lat, lon, t, 1)
            return remote(units.at[unit], dst.at[lon], ssem.at[t], rsem.at[lon], p, q)

        return one

    wo1copy = wcast(3, wo1, w1s, w1r)
    wo2copy = wcast(7, wo2, w2s, w2r)
    sends = lax.rem(lon, 2) == core

    def wbegin(copy, unit, dst, rsem):
        @pl.when(sends)
        def _():
            loop(1, 16, lambda t: copy(t).start())
            pltpu.make_async_copy(units.at[unit], dst.at[lon], rsem.at[lon]).start()

    def wshare(dst, rsem, fsem, k):
        slot = 2 * k + core
        return remote(dst.at[slot], dst.at[slot], fsem.at[k], rsem.at[slot], sib, lon)

    def wforward(dst, rsem, fsem):
        def one(k):
            arrived(dst.at[2 * k + core], rsem.at[2 * k + core]).wait()
            wshare(dst, rsem, fsem, k).start()

        loop(0, 8, one)

    def wrest(dst, rsem):
        loop(0, 8, lambda k: arrived(dst.at[2 * k + 1 - core], rsem.at[2 * k + 1 - core]).wait())

    def u2do(act):
        for i in range(3):
            part, h = head_unit(lon, i)
            slot = part * 8 + lax.rem(h, 8)

            @pl.when(h // 8 == core)
            def _():
                def one(t):
                    p, q = shifted(lat, lon, t, 1)
                    c = remote(units.at[4 + i], u2.at[slot], u2s.at[i, t], u2r.at[slot], p, q)
                    if act == "start":
                        c.start()
                    else:
                        c.wait_send()

                loop(1, 16, one)
                if act == "start":
                    pltpu.make_async_copy(units.at[4 + i], u2.at[slot], u2r.at[slot]).start()

    def u1slot(k, c):
        return (k // 2) * 4 + lax.rem(k, 2) * 2 + c

    def u1share(k):
        slot = u1slot(k, core)
        return remote(u1.at[slot], u1.at[slot], u1f.at[k], u1r.at[slot], sib, lon)

    def u1forward(k):
        slot = u1slot(k, core)
        arrived(u1.at[slot], u1r.at[slot]).wait()
        u1share(k).start()

    loop(0, 6, u1forward)
    wbegin(wo1copy, 3, wo1, w1r)
    loop(1, 16, lambda s: arrived(vl.at[lax.rem(lon + s, 16)], v1r.at[lax.rem(lon + s, 16)]).wait())

    def collect(s):
        src = lax.rem(b + s, 4)
        loop(0, 4, lambda aa: arrived(row.at[src, aa], rr.at[src, aa]).wait())

    loop(1, 4, collect)
    loop(0, 6, lambda k: arrived(u1.at[u1slot(k, 1 - core)], u1r.at[u1slot(k, 1 - core)]).wait())
    u2do("start")

    qkv = nt(u1[...].reshape(576, D), row[...].reshape(1024, D)).astype(BF)
    for h in range(4):
        for qb in range(4):
            q_s[qb, h] = qkv[h * HD : (h + 1) * HD, qb * 256 : (qb + 1) * 256]
        kv_s[h] = qkv[192 + h * HD : 192 + (h + 1) * HD]
        kv_s[4 + h] = qkv[384 + h * HD : 384 + (h + 1) * HD]
    ka1 = jnp.concatenate(
        [vl[(2 * (j % 2)) * 4 + j // 2] + vl[(2 * (j % 2) + 1) * 4 + j // 2] for j in range(8)], axis=1
    )
    o_s[...] = jnp.zeros_like(o_s)

    def ocopy(bb, aa):
        return remote(o_s.at[bb, aa], land_o.at[lon], os.at[bb, aa], orr.at[lon], lat, aa * 4 + bb)

    def block(qb):
        def head(h):
            k_aug = jnp.concatenate([kv_s[h], ka1], axis=0)
            q_aug = jnp.concatenate([q_s[qb, h], qa1[...]], axis=0)
            v_aug = jnp.concatenate([kv_s[4 + h], jnp.ones((16, 1024), BF)], axis=0)
            t_s[h] = soft(k_aug, q_aug, v_aug)

        loop(0, 4, head)
        o = jnp.transpose(t_s[...].reshape(192, 256)).astype(BF)
        for aa in range(4):
            o_s[qb, aa, :, :192] = o[aa * 64 : (aa + 1) * 64]

        def send(aa):
            @pl.when(aa * 4 + qb != lon)
            def _():
                ocopy(qb, aa).start()

        loop(0, 4, send)

    loop(0, 4, block)
    land_o[lon] = o_s[b, a]
    wbegin(wo2copy, 7, wo2, w2r)
    wforward(wo1, w1r, w1f)
    loop(1, 16, lambda s: arrived(land_o.at[lax.rem(lon + s, 16)], orr.at[lax.rem(lon + s, 16)]).wait())
    wrest(wo1, w1r)

    heads = jnp.concatenate(
        [
            jnp.concatenate([land_o[4 * k + g][:, :192] for g in range(4)], axis=1)
            for k in range(4)
        ],
        axis=0,
    )
    middle = start_s[...] + nt(heads, wo1[...].reshape(D, D))
    start_s[...] = middle

    i = lax.broadcasted_iota(jnp.int32, (256, 256), 0)
    j = lax.broadcasted_iota(jnp.int32, (256, 256), 1)
    from_row = ((i >> 2) & 3) * 64 + (i >> 4) * 4 + (i & 3)
    perm = jnp.where(from_row == j, 1.0, 0.0).astype(BF)
    xn2 = jnp.dot(perm, normalize(middle, g2[...]), preferred_element_type=F32).astype(BF)
    x2_s[...] = xn2.reshape(16, 16, D)

    def x2copy(s):
        to = lax.rem(place + s, 16)
        return remote(
            x2_s.at[to], col.at[core, place], x2s.at[s], x2r.at[core, place], to * 2 + core, lon
        )

    def x2share(src):
        return remote(col.at[core, src], col.at[core, src], x2f.at[src], x2r.at[core, src], sib, lon)

    loop(1, 16, lambda s: x2copy(s).start())
    col[core, place] = x2_s[place]
    x2share(place).start()

    def x2forward(s):
        src = lax.rem(place + 16 - s, 16)
        arrived(col.at[core, src], x2r.at[core, src]).wait()
        x2share(src).start()

    loop(1, 16, x2forward)

    def mwait(s):
        src = lax.rem(lat + NLAT - s, NLAT)
        c, p = lax.rem(src, 2), src // 2
        arrived(mv.at[c, p], v2r.at[c, p]).wait()

    loop(1, NLAT, mwait)
    loop(0, 24, lambda k: arrived(u2.at[k], u2r.at[k]).wait())
    loop(0, 16, lambda k: arrived(col.at[1 - core, k], x2r.at[1 - core, k]).wait())

    qkv2[...] = nt(u2[...].reshape(1152, D), col[...].reshape(512, D)).astype(BF).reshape(24, HD, 512)
    ka2 = (nt(e_ref[...], mv[...].reshape(512, 128)) + ka2c[...]).astype(BF)

    def head2(h):
        k_aug = jnp.concatenate([qkv2[8 + h], ka2], axis=0)
        q_aug = jnp.concatenate([qkv2[h], qa2[...]], axis=0)
        v_aug = jnp.concatenate([qkv2[16 + h], jnp.ones((16, 512), BF)], axis=0)
        t2[h] = soft(k_aug, q_aug, v_aug)

    loop(0, 8, head2)
    o2_s[...] = jnp.transpose(t2[...].reshape(384, 512)).astype(BF).reshape(2, 16, 16, 384)

    def bcopy(s):
        to = lax.rem(lat + s, NLAT)
        return remote(
            o2_s.at[lax.rem(to, 2), to // 2], back.at[core, place], bs.at[s], br.at[core, place], to, lon
        )

    loop(1, NLAT, lambda s: bcopy(s).start())
    back[core, place] = o2_s[core, place]
    wforward(wo2, w2r, w2f)

    def bwait(s):
        src = lax.rem(lat + NLAT - s, NLAT)
        c, p = lax.rem(src, 2), src // 2
        arrived(back.at[c, p], br.at[c, p]).wait()

    loop(1, NLAT, bwait)
    wrest(wo2, w2r)
    heads2 = jnp.concatenate([back[0].reshape(256, 384), back[1].reshape(256, 384)], axis=1)
    heads2 = lax.dot_general(
        perm, heads2, (((0,), (0,)), ((), ())), preferred_element_type=F32
    ).astype(BF)
    out[...] = (start_s[...] + nt(heads2, wo2[...].reshape(D, D))).astype(BF)

    loop(1, 16, lambda s: wcopy(s).wait_send())
    sibling.wait_send()
    loop(1, 16, lambda s: v1copy(s).wait_send())
    loop(1, NLAT, lambda s: v2copy(s).wait_send())
    loop(1, 4, lambda s: ycopy(s).wait_send())
    loop(1, 4, lambda s: loop(0, 4, lambda aa: xcopy(s, aa).wait_send()))
    each_u1("finish")
    loop(0, 6, lambda k: u1share(k).wait_send())

    @pl.when(sends)
    def _():
        loop(1, 16, lambda t: wo1copy(t).wait_send())
        loop(1, 16, lambda t: wo2copy(t).wait_send())

    loop(0, 8, lambda k: wshare(wo1, w1r, w1f, k).wait_send())
    loop(0, 8, lambda k: wshare(wo2, w2r, w2f, k).wait_send())
    u2do("finish")

    def osent(k):
        bb, aa = lax.rem(k, 4), k // 4

        @pl.when(k != lon)
        def _():
            ocopy(bb, aa).wait_send()

    loop(0, 16, osent)
    loop(1, 16, lambda s: x2copy(s).wait_send())
    loop(0, 16, lambda k: x2share(k).wait_send())
    loop(1, NLAT, lambda s: bcopy(s).wait_send())


def pair(*args):
    return pl.pallas_call(
        pair_kernel,
        out_shape=jax.ShapeDtypeStruct((256, D), BF),
        in_specs=[VMEM] * len(args),
        out_specs=VMEM,
        scratch_shapes=[
            pltpu.VMEM((2, 16, 24, 384), BF),
            pltpu.VMEM((8, HD, D), BF),
            pltpu.VMEM((256, D), F32),
            pltpu.VMEM((4, 64, D), BF),
            pltpu.VMEM((4, 4, 64, D), BF),
            pltpu.VMEM((12, HD, D), BF),
            pltpu.VMEM((16, HD, D), BF),
            pltpu.VMEM((24, HD, D), BF),
            pltpu.VMEM((16, HD, D), BF),
            pltpu.VMEM((16, 16, 128), BF),
            pltpu.VMEM((2, 16, 16, 128), BF),
            pltpu.VMEM((4, 4, HD, 256), BF),
            pltpu.VMEM((8, HD, 1024), BF),
            pltpu.VMEM((4, HD, 256), F32),
            pltpu.VMEM((4, 4, 64, 256), BF),
            pltpu.VMEM((16, 64, 256), BF),
            pltpu.VMEM((16, 16, D), BF),
            pltpu.VMEM((2, 16, 16, D), BF),
            pltpu.VMEM((24, HD, 512), BF),
            pltpu.VMEM((8, HD, 512), F32),
            pltpu.VMEM((2, 16, 16, 384), BF),
            pltpu.VMEM((2, 16, 16, 384), BF),
            DMA((16,)), DMA((16,)), DMA, DMA, DMA((16,)), DMA((16,)), DMA((NLAT,)), DMA((2, 16)),
            DMA((4,)), DMA((4, 4)), DMA((4, 4)), DMA((3, 4)), DMA((12,)), DMA((6,)),
            DMA((16,)), DMA((16,)), DMA((8,)), DMA((3, 16)), DMA((24,)),
            DMA((16,)), DMA((16,)), DMA((8,)), DMA((4, 4)), DMA((16,)),
            DMA((16,)), DMA((2, 16)), DMA((16,)), DMA((NLAT,)), DMA((2, 16)),
        ],
        compiler_params=pltpu.CompilerParams(
            collective_id=0, has_side_effects=True, vmem_limit_bytes=LIMIT
        ),
    )(*args)


def local(
    tokens, source_id, valid, source_table, gain_lon, gain_lat, wqkv_lon, wout_lon, wqkv_lat, wout_lat
):
    rows, cols, width = tokens.shape
    lat, lon = where_am_i()
    shard = jnp.concatenate([wqkv_lon, wout_lon, wqkv_lat, wout_lat], axis=1)
    bias = jnp.where(valid > 0, 0.0, -1e30).astype(BF)
    low = jnp.pad(bias, ((0, 0), (0, 64)))
    high = jnp.pad(bias, ((0, 0), (64, 0)))
    v1 = jnp.where((lon // 4) % 2 == 0, low, high)[:, None, :]
    v1 = jnp.pad(v1, ((0, 0), (0, 15), (0, 0)))
    v2 = bias.reshape(4, 16, 4).transpose(1, 0, 2).reshape(16, 16, 1)
    v2 = jnp.pad(v2, ((0, 0), (0, 0), (0, 127)))
    e = jnp.zeros((16, 128), F32).at[0, 0].set(1.0).astype(BF)
    qa1 = jnp.zeros((16, 256), F32).at[0].set(1.0).astype(BF)
    r = lax.broadcasted_iota(jnp.int32, (16, 512), 0)
    same = (lax.broadcasted_iota(jnp.int32, (16, 512), 1) % 4) == r - 1
    column = (r >= 1) & (r <= 4)
    ka2 = jnp.where(same, 1.0, 0.0)
    qa2 = jnp.where(r == 0, 1.0, jnp.where(column & ~same, -1e34, 0.0)).astype(BF)
    mixed = pair(
        shard,
        tokens.reshape(rows * cols, width),
        source_id.reshape(1, rows * cols),
        jnp.pad(source_table, ((0, 3), (0, 0))),
        gain_lon.reshape(1, width),
        gain_lat.reshape(1, width),
        v1,
        v2,
        e,
        qa1,
        ka2,
        qa2,
    )
    return mixed.reshape(rows, cols, width)


def solution(mesh):
    placed = (
        P("lat", "lon", None),
        P("lat", "lon"),
        P("lat", "lon"),
        P(),
        P(),
        P(),
        P("lat", "lon"),
        P("lat", "lon"),
        P("lat", "lon"),
        P("lat", "lon"),
    )
    return jax.shard_map(
        local, mesh=mesh, in_specs=placed, out_specs=P("lat", "lon", None), check_vma=False
    )
```

time: 559 us -> 157 us (0.28); the launches traced: 551 us -> 156 us
  waiting for transfers between devices: 210 us -> 0 us
  blocking collectives: 175 us -> 0 us
  Pallas kernels: 0 us -> 147 us
  local copies, waits for them, and re-layouts: 64.5 us -> 7.94 us
  starting transfers between devices: 52.8 us -> 0 us
  matrix products: 33.4 us -> 0 us
  between operations: 14.2 us -> 0.05 us
    pallas_call x0 -> x1, Pallas kernels: none -> 147 us  [pair(): pl.pallas_call(pair_kernel, out_shape=jax.ShapeDtypeStruct((256, D), BF),...]
    all_gather x4 -> x0, waiting for transfers between devices: 144 us -> none  [the longest x2 99.1 us: fetch(): lax.all_gather(weights[0], 'lat', axis=0, tiled=True)]
    all_gather x4 -> x0, blocking collectives: 143 us -> none  [the longest x2 76.6 us: fetch(): lax.all_gather(weights[0], 'lon', axis=1, tiled=True)]
    all_to_all x9 -> x0, waiting for transfers between devices: 65.7 us -> none  [the longest x1 14.8 us: local(): lax.all_to_all(keys, 'lon', split_axis=2, concat_axis=1, tiled=True)]
    all_to_all x9 -> x0, starting transfers between devices: 52.7 us -> none  [the longest x1 8.63 us: local(): lax.all_to_all(valid, 'lat', split_axis=1, concat_axis=0, tiled=True)]
    all_to_all x1 -> x0, blocking collectives: 32.5 us -> none  [local(): lax.all_to_all(column_out, 'lat', split_axis=0, concat_axis=1, tiled=True)]
    unnamed x52 -> x19, local copies, waits for them, and re-layouts: 31.5 us -> 3.86 us
    dot_general x8 -> x0, matrix products: 23.3 us -> none  [the longest x2 9.96 us: attend(): jnp.einsum(form_out, probs, values, preferred_element_type=jnp.float32)]
  transfers between devices with their start and end apart: 13 -> 0, of which waited for: 9 -> 0; matrix products, arithmetic and copies ran while one was open for 17% -> 0% of each run, Pallas kernels for 0% -> 0%
where the time goes in v2:
time: 157 us; the launch traced here: 156 us
  Pallas kernels  147 us (94%)
  local copies, waits for them, and re-layouts  7.94 us (5%)
    pallas_call x1, Pallas kernels, pair(): pl.pallas_call(pair_kernel, out_shape=jax.ShapeDtypeStruct((256, D), BF),...  147 us
    unnamed x19, local copies, waits for them, and re-layouts  3.86 us

profile of v2, /device:TPU:1, one launch (start us, length us, event | category | flops | bytes accessed | tf_op | source)
XLA Modules:
  0.0 156.4 jit_solution(7810788932632049785)
XLA Ops:
  0.0 0.0 copy-start.7
  0.0 0.7 copy-done.7
  0.7 0.1 select_bitcast_fusion
  0.8 0.0 copy-start.8
  0.8 0.7 copy-done.8
  1.4 0.0 copy-start.5
  1.4 0.7 reshape.72.sid
  2.1 0.0 copy-start.6
  2.1 0.0 copy-done.5
  2.1 0.6 reshape.73.g1
  2.7 0.1 copy-done.6
  2.8 0.6 reshape.74.g2
  3.4 0.6 pad.31.v1
  4.0 0.0 copy-start.2
  4.0 0.0 copy-start.4
  4.0 0.1 reshape.75
  4.1 0.0 copy-start.1
  4.1 0.0 copy-start.3
  4.1 0.1 copy.13
  4.2 0.5 copy-done.2
  4.7 0.0 copy-done.4
  4.7 0.1 copy-done.1
  4.8 0.0 copy-done.3
  4.8 0.0 copy-start
  4.8 0.7 pad_maximum_fusion.shard
  5.5 0.1 copy-done
  5.5 0.6 pad.28.table
  6.2 0.7 select_convert_fusion
  6.8 0.2 copy.14
  7.0 0.6 pad.32.v2
  7.7 146.9 %shard_map.100 = bf16[256,768]{1,0:T(8,128)(2,1)} custom-call(bf16[24,384]{1,0:T(8,128)(2,1)} %pad_maximum_fusion.shard, bf16[256,768]{1,0:T(8,128)(2,1)} %bitcast.7, s32[1,256]{1,0:T(1,128)} %reshape.72.sid, f32[8,768]{1,0:T(8,128)} %pad.28.table, f32[1,768]{1,0:T(1,128)} %reshape.73.g1, f32[1,768]{1,0:T(1,128)} %reshape.74.g2, ...), custom_call_target="tpu_custom_call" | custom-call | tf_op jit(solution)/shard_map/pallas_call | solution.py:430
  154.6 1.8 %copy.16 = bf16[4,64,768]{2,1,0:T(8,128)(2,1)} copy(bf16[4,64,768]{2,1,0:T(8,128)(2,1)} %bitcast.6) | data formatting | bytes 786432
  (6 shorter events, 0.0 us)
Async XLA Ops:
  0.0 0.7 copy-start.7
  0.8 0.7 copy-start.8
  1.4 0.7 copy-start.5
  2.1 0.7 copy-start.6
  4.0 0.7 copy-start.2
  4.0 0.7 copy-start.4
  4.1 0.7 copy-start.1
  4.1 0.7 copy-start.3
  4.8 0.7 copy-start

commit v3 on v2

--- a/solution.py
+++ b/solution.py
@@ -82,16 +82,21 @@
     return o[:HD] / o[HD : HD + 1]
 
 
+def iota(shape, axis):
+    return lax.broadcasted_iota(jnp.int32, shape, axis)
+
+
 def arrived(ref, sem):
     return pltpu.make_async_copy(ref, ref, sem)
 
 
 def pair_kernel(
-    shard, tok, sid, table, g1, g2, v1, v2, e_ref, qa1, ka2c, qa2, out,
+    tok, sid, valid, table, g1, g2, wq1, wp1, wq2, wp2, out,
+    shard, table_s, v1, v2,
     land, units, start_s, xn_s, row, u1, wo1, u2, wo2, vl, mv, q_s, kv_s, t_s, o_s, land_o,
     x2_s, col, qkv2, t2, o2_s, back,
     s1s, s1r, sbs, sbr, v1s, v1r, v2s, v2r, ys, xs, rr, u1s, u1r, u1f, w1s, w1r, w1f, u2s, u2r,
-    w2s, w2r, w2f, os, orr, x2s, x2r, x2f, bs, br,
+    u2f, w2s, w2r, w2f, os, orr, x2s, x2r, x2f, bs, br,
 ):
     lat, lon = where_am_i()
     a, b = lon // 4, lax.rem(lon, 4)
@@ -107,6 +112,37 @@
         signal(bar, lat, lax.rem(lon + t, NLON))
 
     loop(1, 16, greet)
+
+    shard[...] = jnp.concatenate(
+        [w[...].astype(F32) for w in (wq1, wp1, wq2, wp2)], axis=1
+    ).astype(BF)
+    table_s[...] = jnp.zeros_like(table_s)
+    table_s[0:5] = table[...]
+    ids = sid[...]
+    bias = jnp.where(valid[...] > 0, 0.0, -1e30)
+    for k in range(4):
+        onehot = jnp.where(iota((8, 64), 0) == ids[k : k + 1], 1.0, 0.0)
+        emb = lax.dot_general(
+            onehot, table_s[...], (((0,), (0,)), ((), ())),
+            precision=lax.Precision.HIGHEST, preferred_element_type=F32,
+        )
+        first = tok[k].astype(F32) + emb
+        start_s[k * 64 : (k + 1) * 64] = first
+        xn_s[k] = normalize(first, g1[...].reshape(1, D))
+        line = jnp.where(iota((16, 64), 0) == 0, bias[k : k + 1], 0.0)
+        none = jnp.zeros((16, 64), F32)
+        v1[k] = jnp.where(
+            lax.rem(a, 2) == 0,
+            jnp.concatenate([line, none], axis=1),
+            jnp.concatenate([none, line], axis=1),
+        ).astype(BF)
+    token, lane = iota((256, 64), 0), iota((256, 64), 1)
+    picks = jnp.where((token >> 4) * 4 + (token & 3) == lane, 1.0, 0.0).astype(BF)
+    tall = jnp.concatenate([bias, jnp.zeros((124, 64), F32)], axis=0).astype(BF)
+    v2all = nt(picks, tall)
+    v2all = jnp.where(iota((256, 128), 1) == ((iota((256, 128), 0) >> 2) & 3), v2all, 0.0)
+    v2[...] = v2all.astype(BF).reshape(16, 16, 128)
+
     pl.semaphore_wait(bar, 61)
 
     def wcopy(s):
@@ -116,15 +152,6 @@
     loop(1, 16, lambda s: wcopy(s).start())
     land[core, place] = shard[...]
 
-    kind = lax.broadcasted_iota(jnp.int32, (8, 256), 0)
-    onehot = jnp.where(kind == sid[...], 1.0, 0.0)
-    emb = lax.dot_general(
-        onehot, table[...], (((0,), (0,)), ((), ())),
-        precision=lax.Precision.HIGHEST, preferred_element_type=F32,
-    )
-    start = tok[...].astype(F32) + emb
-    start_s[...] = start
-    xn_s[...] = normalize(start, g1[...]).reshape(4, 64, D)
 
     def ycopy(s):
         to = lax.rem(a + s, 4)
@@ -236,7 +263,10 @@
             part, h = head_unit(lon, i)
             slot = part * 8 + lax.rem(h, 8)
 
-            @pl.when(h // 8 == core)
+            here = h // 8 == core
+            here = here if i == 0 else here & (lax.rem(place, 2) == i - 1)
+
+            @pl.when(here)
             def _():
                 def one(t):
                     p, q = shifted(lat, lon, t, 1)
@@ -249,6 +279,31 @@
                 loop(1, 16, one)
                 if act == "start":
                     pltpu.make_async_copy(units.at[4 + i], u2.at[slot], u2r.at[slot]).start()
+
+    zsib = lat + 2 - 4 * lax.rem(place, 2)
+
+    def u2class(k):
+        return lax.rem((k // 8) * 16 + core * 8 + lax.rem(k, 8), 3)
+
+    def u2share(k):
+        return remote(u2.at[k], u2.at[k], u2f.at[k], u2r.at[k], zsib, lon)
+
+    def u2pass(act):
+        def one(k):
+            @pl.when(u2class(k) == 1 + lax.rem(place, 2))
+            def _():
+                if act == "start":
+                    arrived(u2.at[k], u2r.at[k]).wait()
+                    u2share(k).start()
+                else:
+                    u2share(k).wait_send()
+
+        loop(0, 24, one)
+
+    def u2rest(k):
+        @pl.when(u2class(k) != 1 + lax.rem(place, 2))
+        def _():
+            arrived(u2.at[k], u2r.at[k]).wait()
 
     def u1slot(k, c):
         return (k // 2) * 4 + lax.rem(k, 2) * 2 + c
@@ -283,6 +338,7 @@
     ka1 = jnp.concatenate(
         [vl[(2 * (j % 2)) * 4 + j // 2] + vl[(2 * (j % 2) + 1) * 4 + j // 2] for j in range(8)], axis=1
     )
+    qa1 = jnp.where(iota((16, 256), 0) == 0, 1.0, 0.0).astype(BF)
     o_s[...] = jnp.zeros_like(o_s)
 
     def ocopy(bb, aa):
@@ -291,7 +347,7 @@
     def block(qb):
         def head(h):
             k_aug = jnp.concatenate([kv_s[h], ka1], axis=0)
-            q_aug = jnp.concatenate([q_s[qb, h], qa1[...]], axis=0)
+            q_aug = jnp.concatenate([q_s[qb, h], qa1], axis=0)
             v_aug = jnp.concatenate([kv_s[4 + h], jnp.ones((16, 1024), BF)], axis=0)
             t_s[h] = soft(k_aug, q_aug, v_aug)
 
@@ -309,8 +365,8 @@
 
     loop(0, 4, block)
     land_o[lon] = o_s[b, a]
-    wbegin(wo2copy, 7, wo2, w2r)
     wforward(wo1, w1r, w1f)
+    u2pass("start")
     loop(1, 16, lambda s: arrived(land_o.at[lax.rem(lon + s, 16)], orr.at[lax.rem(lon + s, 16)]).wait())
     wrest(wo1, w1r)
 
@@ -328,7 +384,7 @@
     j = lax.broadcasted_iota(jnp.int32, (256, 256), 1)
     from_row = ((i >> 2) & 3) * 64 + (i >> 4) * 4 + (i & 3)
     perm = jnp.where(from_row == j, 1.0, 0.0).astype(BF)
-    xn2 = jnp.dot(perm, normalize(middle, g2[...]), preferred_element_type=F32).astype(BF)
+    xn2 = jnp.dot(perm, normalize(middle, g2[...].reshape(1, D)), preferred_element_type=F32).astype(BF)
     x2_s[...] = xn2.reshape(16, 16, D)
 
     def x2copy(s):
@@ -350,6 +406,7 @@
         x2share(src).start()
 
     loop(1, 16, x2forward)
+    wbegin(wo2copy, 7, wo2, w2r)
 
     def mwait(s):
         src = lax.rem(lat + NLAT - s, NLAT)
@@ -357,15 +414,20 @@
         arrived(mv.at[c, p], v2r.at[c, p]).wait()
 
     loop(1, NLAT, mwait)
-    loop(0, 24, lambda k: arrived(u2.at[k], u2r.at[k]).wait())
+    loop(0, 24, u2rest)
     loop(0, 16, lambda k: arrived(col.at[1 - core, k], x2r.at[1 - core, k]).wait())
 
     qkv2[...] = nt(u2[...].reshape(1152, D), col[...].reshape(512, D)).astype(BF).reshape(24, HD, 512)
-    ka2 = (nt(e_ref[...], mv[...].reshape(512, 128)) + ka2c[...]).astype(BF)
+    first = jnp.where((iota((16, 128), 0) == 0) & (iota((16, 128), 1) < 4), 1.0, 0.0).astype(BF)
+    fr = iota((16, 512), 0)
+    same = (iota((16, 512), 1) & 3) == fr - 1
+    ka2 = (nt(first, mv[...].reshape(512, 128)) + jnp.where(same, 1.0, 0.0)).astype(BF)
+    other = (fr >= 1) & (fr <= 4) & jnp.logical_not(same)
+    qa2 = jnp.where(fr == 0, 1.0, jnp.where(other, -1e34, 0.0)).astype(BF)
 
     def head2(h):
         k_aug = jnp.concatenate([qkv2[8 + h], ka2], axis=0)
-        q_aug = jnp.concatenate([qkv2[h], qa2[...]], axis=0)
+        q_aug = jnp.concatenate([qkv2[h], qa2], axis=0)
         v_aug = jnp.concatenate([qkv2[16 + h], jnp.ones((16, 512), BF)], axis=0)
         t2[h] = soft(k_aug, q_aug, v_aug)
 
@@ -393,7 +455,7 @@
     heads2 = lax.dot_general(
         perm, heads2, (((0,), (0,)), ((), ())), preferred_element_type=F32
     ).astype(BF)
-    out[...] = (start_s[...] + nt(heads2, wo2[...].reshape(D, D))).astype(BF)
+    out[...] = (start_s[...] + nt(heads2, wo2[...].reshape(D, D))).astype(BF).reshape(4, 64, D)
 
     loop(1, 16, lambda s: wcopy(s).wait_send())
     sibling.wait_send()
@@ -412,6 +474,7 @@
     loop(0, 8, lambda k: wshare(wo1, w1r, w1f, k).wait_send())
     loop(0, 8, lambda k: wshare(wo2, w2r, w2f, k).wait_send())
     u2do("finish")
+    u2pass("finish")
 
     def osent(k):
         bb, aa = lax.rem(k, 4), k // 4
@@ -429,10 +492,14 @@
 def pair(*args):
     return pl.pallas_call(
         pair_kernel,
-        out_shape=jax.ShapeDtypeStruct((256, D), BF),
+        out_shape=jax.ShapeDtypeStruct((4, 64, D), BF),
         in_specs=[VMEM] * len(args),
         out_specs=VMEM,
         scratch_shapes=[
+            pltpu.VMEM((24, 384), BF),
+            pltpu.VMEM((8, D), F32),
+            pltpu.VMEM((4, 16, 128), BF),
+            pltpu.VMEM((16, 16, 128), BF),
             pltpu.VMEM((2, 16, 24, 384), BF),
             pltpu.VMEM((8, HD, D), BF),
             pltpu.VMEM((256, D), F32),
@@ -457,7 +524,7 @@
             pltpu.VMEM((2, 16, 16, 384), BF),
             DMA((16,)), DMA((16,)), DMA, DMA, DMA((16,)), DMA((16,)), DMA((NLAT,)), DMA((2, 16)),
             DMA((4,)), DMA((4, 4)), DMA((4, 4)), DMA((3, 4)), DMA((12,)), DMA((6,)),
-            DMA((16,)), DMA((16,)), DMA((8,)), DMA((3, 16)), DMA((24,)),
+            DMA((16,)), DMA((16,)), DMA((8,)), DMA((3, 16)), DMA((24,)), DMA((24,)),
             DMA((16,)), DMA((16,)), DMA((8,)), DMA((4, 4)), DMA((16,)),
             DMA((16,)), DMA((2, 16)), DMA((16,)), DMA((NLAT,)), DMA((2, 16)),
         ],
@@ -470,38 +537,9 @@
 def local(
     tokens, source_id, valid, source_table, gain_lon, gain_lat, wqkv_lon, wout_lon, wqkv_lat, wout_lat
 ):
-    rows, cols, width = tokens.shape
-    lat, lon = where_am_i()
-    shard = jnp.concatenate([wqkv_lon, wout_lon, wqkv_lat, wout_lat], axis=1)
-    bias = jnp.where(valid > 0, 0.0, -1e30).astype(BF)
-    low = jnp.pad(bias, ((0, 0), (0, 64)))
-    high = jnp.pad(bias, ((0, 0), (64, 0)))
-    v1 = jnp.where((lon // 4) % 2 == 0, low, high)[:, None, :]
-    v1 = jnp.pad(v1, ((0, 0), (0, 15), (0, 0)))
-    v2 = bias.reshape(4, 16, 4).transpose(1, 0, 2).reshape(16, 16, 1)
-    v2 = jnp.pad(v2, ((0, 0), (0, 0), (0, 127)))
-    e = jnp.zeros((16, 128), F32).at[0, 0].set(1.0).astype(BF)
-    qa1 = jnp.zeros((16, 256), F32).at[0].set(1.0).astype(BF)
-    r = lax.broadcasted_iota(jnp.int32, (16, 512), 0)
-    same = (lax.broadcasted_iota(jnp.int32, (16, 512), 1) % 4) == r - 1
-    column = (r >= 1) & (r <= 4)
-    ka2 = jnp.where(same, 1.0, 0.0)
-    qa2 = jnp.where(r == 0, 1.0, jnp.where(column & ~same, -1e34, 0.0)).astype(BF)
-    mixed = pair(
-        shard,
-        tokens.reshape(rows * cols, width),
-        source_id.reshape(1, rows * cols),
-        jnp.pad(source_table, ((0, 3), (0, 0))),
-        gain_lon.reshape(1, width),
-        gain_lat.reshape(1, width),
-        v1,
-        v2,
-        e,
-        qa1,
-        ka2,
-        qa2,
+    return pair(
+        tokens, source_id, valid, source_table, gain_lon, gain_lat, wqkv_lon, wout_lon, wqkv_lat, wout_lat
     )
-    return mixed.reshape(rows, cols, width)
 
 
 def solution(mesh):

time: 157 us -> 139 us (0.89)
  the two profiles are of different devices: /device:TPU:1 before, /device:TPU:31 now
where the time goes in v3:
time: 139 us
  Pallas kernels  137 us (99%)
  local copies, waits for them, and re-layouts  1.77 us (1%)
    pallas_call x1, Pallas kernels, pair(): pl.pallas_call(pair_kernel, out_shape=jax.ShapeDtypeStruct((4, 64, D), BF...  137 us

profile of v3, /device:TPU:31, one launch (start us, length us, event | category | flops | bytes accessed | tf_op | source)
XLA Modules:
  0.0 138.9 jit_solution(6714043648531530110)
XLA Ops:
  0.0 137.1 %shard_map.100 = bf16[4,64,768]{2,1,0:T(8,128)(2,1)} custom-call(bf16[4,64,768]{2,1,0:T(8,128)(2,1)} %tok.1, s32[4,64]{1,0:T(4,128)} %sid.1, s32[4,64]{1,0:T(4,128)} %valid.1, f32[5,768]{1,0:T(8,128)} %table.1, f32[768]{0:T(1024)} %g1.1, f32[768]{0:T(1024)} %g2.1, bf16[24,144]{1,0:T(8,128)(2,1)} %wq1.1, bf16[24,48]{1,0:T(8,128)(2,1)} %wp1.1, ...), custom_call_target="tpu_custom_call" | custom-call | tf_op jit(solution)/shard_map/pallas_call | solution.py:493
  137.1 1.8 %copy.12 = bf16[4,64,768]{2,1,0:T(8,128)(2,1)} copy(bf16[4,64,768]{2,1,0:T(8,128)(2,1)} %shard_map.100) | data formatting | bytes 786432

commit v4 on v3

--- a/solution.py
+++ b/solution.py
@@ -116,10 +116,26 @@
     shard[...] = jnp.concatenate(
         [w[...].astype(F32) for w in (wq1, wp1, wq2, wp2)], axis=1
     ).astype(BF)
+    land[core, place] = shard[...]
+    pl.semaphore_wait(bar, 61)
+
+    def wcopy(s):
+        to = lax.rem(place + s, 16)
+        return remote(shard, land.at[core, place], s1s.at[s], s1r.at[place], to * 2 + core, lon)
+
+    loop(1, 16, lambda s: wcopy(s).start())
+
+    def ycopy(s):
+        to = lax.rem(a + s, 4)
+        return remote(xn_s.at[to], row.at[b, a], ys.at[s], rr.at[b, a], lat, to * 4 + b)
+
+    def xcopy(s, aa):
+        to = lax.rem(b + s, 4)
+        return remote(row.at[b, aa], row.at[b, aa], xs.at[s, aa], rr.at[b, aa], lat, a * 4 + to)
+
     table_s[...] = jnp.zeros_like(table_s)
     table_s[0:5] = table[...]
     ids = sid[...]
-    bias = jnp.where(valid[...] > 0, 0.0, -1e30)
     for k in range(4):
         onehot = jnp.where(iota((8, 64), 0) == ids[k : k + 1], 1.0, 0.0)
         emb = lax.dot_general(
@@ -129,6 +145,13 @@
         first = tok[k].astype(F32) + emb
         start_s[k * 64 : (k + 1) * 64] = first
         xn_s[k] = normalize(first, g1[...].reshape(1, D))
+
+    loop(1, 4, lambda s: ycopy(s).start())
+    row[b, a] = xn_s[a]
+    loop(1, 4, lambda s: xcopy(s, a).start())
+
+    bias = jnp.where(valid[...] > 0, 0.0, -1e30)
+    for k in range(4):
         line = jnp.where(iota((16, 64), 0) == 0, bias[k : k + 1], 0.0)
         none = jnp.zeros((16, 64), F32)
         v1[k] = jnp.where(
@@ -143,28 +166,6 @@
     v2all = jnp.where(iota((256, 128), 1) == ((iota((256, 128), 0) >> 2) & 3), v2all, 0.0)
     v2[...] = v2all.astype(BF).reshape(16, 16, 128)
 
-    pl.semaphore_wait(bar, 61)
-
-    def wcopy(s):
-        to = lax.rem(place + s, 16)
-        return remote(shard, land.at[core, place], s1s.at[s], s1r.at[place], to * 2 + core, lon)
-
-    loop(1, 16, lambda s: wcopy(s).start())
-    land[core, place] = shard[...]
-
-
-    def ycopy(s):
-        to = lax.rem(a + s, 4)
-        return remote(xn_s.at[to], row.at[b, a], ys.at[s], rr.at[b, a], lat, to * 4 + b)
-
-    def xcopy(s, aa):
-        to = lax.rem(b + s, 4)
-        return remote(row.at[b, aa], row.at[b, aa], xs.at[s, aa], rr.at[b, aa], lat, a * 4 + to)
-
-    loop(1, 4, lambda s: ycopy(s).start())
-    row[b, a] = xn_s[a]
-    loop(1, 4, lambda s: xcopy(s, a).start())
-
     def v1copy(s):
         to = lax.rem(lon + s, NLON)
         return remote(v1.at[to // 4], vl.at[lon], v1s.at[s], v1r.at[lon], lat, to)
@@ -227,21 +228,51 @@
 
     each_u1("start")
 
-    def wcast(unit, dst, ssem, rsem):
-        def one(t):
-            p, q = shifted(lat, lon, t, 1)
-            return remote(units.at[unit], dst.at[lon], ssem.at[t], rsem.at[lon], p, q)
-
-        return one
-
-    wo1copy = wcast(3, wo1, w1s, w1r)
-    wo2copy = wcast(7, wo2, w2s, w2r)
-    sends = lax.rem(lon, 2) == core
-
-    def wbegin(copy, unit, dst, rsem):
+    sends = lax.rem(b, 2) == core
+
+    def xpeer(s):
+        return a * 4 + lax.rem(b + s, 4)
+
+    def wcast(unit, dst, ssem, rsem, act):
         @pl.when(sends)
         def _():
-            loop(1, 16, lambda t: copy(t).start())
+            def along_y(d):
+                p, q = shifted(lat, lon, 4 * d, 1)
+                c = remote(units.at[unit], dst.at[lon], ssem.at[0, d], rsem.at[lon], p, q)
+                act(c)
+
+            def along_x(k):
+                c = remote(units.at[unit], dst.at[lon], ssem.at[k, 0], rsem.at[lon], lat, xpeer(k))
+                act(c)
+
+            loop(1, 4, along_y)
+            loop(1, 4, along_x)
+
+    def wpass(dst, ssem, rsem, act, wait):
+        @pl.when(sends)
+        def _():
+            def one(d):
+                slot = lax.rem(a + d, 4) * 4 + b
+                if wait:
+                    arrived(dst.at[slot], rsem.at[slot]).wait()
+                loop(
+                    1, 4,
+                    lambda k: act(remote(dst.at[slot], dst.at[slot], ssem.at[k, d], rsem.at[slot], lat, xpeer(k))),
+                )
+
+            loop(1, 4, one)
+
+    def go(c):
+        c.start()
+
+    def left(c):
+        c.wait_send()
+
+    def wbegin(unit, dst, ssem, rsem):
+        wcast(unit, dst, ssem, rsem, go)
+
+        @pl.when(sends)
+        def _():
             pltpu.make_async_copy(units.at[unit], dst.at[lon], rsem.at[lon]).start()
 
     def wshare(dst, rsem, fsem, k):
@@ -250,7 +281,12 @@
 
     def wforward(dst, rsem, fsem):
         def one(k):
-            arrived(dst.at[2 * k + core], rsem.at[2 * k + core]).wait()
+            slot = 2 * k + core
+
+            @pl.when(jnp.logical_not((lax.rem(slot, 4) == b) & (slot // 4 != a)))
+            def _():
+                arrived(dst.at[slot], rsem.at[slot]).wait()
+
             wshare(dst, rsem, fsem, k).start()
 
         loop(0, 8, one)
@@ -258,52 +294,81 @@
     def wrest(dst, rsem):
         loop(0, 8, lambda k: arrived(dst.at[2 * k + 1 - core], rsem.at[2 * k + 1 - core]).wait())
 
+    def u2slot(j, i):
+        u = j * 3 + i
+        part, h = u // 16, lax.rem(u, 16)
+        here = h // 8 == core
+        here = here if i == 0 else here & (lax.rem(place, 2) == i - 1)
+        return here, part * 8 + lax.rem(h, 8)
+
     def u2do(act):
         for i in range(3):
-            part, h = head_unit(lon, i)
-            slot = part * 8 + lax.rem(h, 8)
-
-            here = h // 8 == core
-            here = here if i == 0 else here & (lax.rem(place, 2) == i - 1)
+            here, slot = u2slot(lon, i)
 
             @pl.when(here)
             def _():
-                def one(t):
-                    p, q = shifted(lat, lon, t, 1)
-                    c = remote(units.at[4 + i], u2.at[slot], u2s.at[i, t], u2r.at[slot], p, q)
-                    if act == "start":
-                        c.start()
-                    else:
-                        c.wait_send()
-
-                loop(1, 16, one)
-                if act == "start":
+                def along_y(d):
+                    p, q = shifted(lat, lon, 4 * d, 1)
+                    act(remote(units.at[4 + i], u2.at[slot], u2s.at[i, 0, d], u2r.at[slot], p, q))
+
+                def along_x(k):
+                    act(remote(units.at[4 + i], u2.at[slot], u2s.at[i, k, 0], u2r.at[slot], lat, xpeer(k)))
+
+                loop(1, 4, along_y)
+                loop(1, 4, along_x)
+                if act is go:
                     pltpu.make_async_copy(units.at[4 + i], u2.at[slot], u2r.at[slot]).start()
+
+    def u2on(act):
+        def one(d):
+            for i in range(3):
+                here, slot = u2slot(lax.rem(a + d, 4) * 4 + b, i)
+
+                @pl.when(here)
+                def _():
+                    if act is go:
+                        arrived(u2.at[slot], u2r.at[slot]).wait()
+                    loop(
+                        1, 4,
+                        lambda k: act(remote(u2.at[slot], u2.at[slot], u2s.at[i, k, d], u2r.at[slot], lat, xpeer(k))),
+                    )
+
+        loop(1, 4, one)
 
     zsib = lat + 2 - 4 * lax.rem(place, 2)
 
     def u2class(k):
         return lax.rem((k // 8) * 16 + core * 8 + lax.rem(k, 8), 3)
 
+    def u2early(k):
+        j = ((k // 8) * 16 + core * 8 + lax.rem(k, 8)) // 3
+        here = u2class(k) != 2 - lax.rem(place, 2)
+        return here & (lax.rem(j, 4) == b) & (j // 4 != a)
+
+    def u2wait(k):
+        @pl.when(jnp.logical_not(u2early(k)))
+        def _():
+            arrived(u2.at[k], u2r.at[k]).wait()
+
     def u2share(k):
         return remote(u2.at[k], u2.at[k], u2f.at[k], u2r.at[k], zsib, lon)
 
-    def u2pass(act):
+    def u2pass(act, lo=0, hi=24):
         def one(k):
             @pl.when(u2class(k) == 1 + lax.rem(place, 2))
             def _():
                 if act == "start":
-                    arrived(u2.at[k], u2r.at[k]).wait()
+                    u2wait(k)
                     u2share(k).start()
                 else:
                     u2share(k).wait_send()
 
-        loop(0, 24, one)
+        loop(lo, hi, one)
 
     def u2rest(k):
         @pl.when(u2class(k) != 1 + lax.rem(place, 2))
         def _():
-            arrived(u2.at[k], u2r.at[k]).wait()
+            u2wait(k)
 
     def u1slot(k, c):
         return (k // 2) * 4 + lax.rem(k, 2) * 2 + c
@@ -317,8 +382,10 @@
         arrived(u1.at[slot], u1r.at[slot]).wait()
         u1share(k).start()
 
+    u2do(go)
     loop(0, 6, u1forward)
-    wbegin(wo1copy, 3, wo1, w1r)
+    u2on(go)
+    wbegin(3, wo1, w1s, w1r)
     loop(1, 16, lambda s: arrived(vl.at[lax.rem(lon + s, 16)], v1r.at[lax.rem(lon + s, 16)]).wait())
 
     def collect(s):
@@ -327,7 +394,6 @@
 
     loop(1, 4, collect)
     loop(0, 6, lambda k: arrived(u1.at[u1slot(k, 1 - core)], u1r.at[u1slot(k, 1 - core)]).wait())
-    u2do("start")
 
     qkv = nt(u1[...].reshape(576, D), row[...].reshape(1024, D)).astype(BF)
     for h in range(4):
@@ -362,11 +428,16 @@
                 ocopy(qb, aa).start()
 
         loop(0, 4, send)
+        u2pass("start", qb * 6, qb * 6 + 6)
+
+        @pl.when(qb == 1)
+        def _():
+            wpass(wo1, w1s, w1r, go, True)
+
 
     loop(0, 4, block)
     land_o[lon] = o_s[b, a]
     wforward(wo1, w1r, w1f)
-    u2pass("start")
     loop(1, 16, lambda s: arrived(land_o.at[lax.rem(lon + s, 16)], orr.at[lax.rem(lon + s, 16)]).wait())
     wrest(wo1, w1r)
 
@@ -406,7 +477,7 @@
         x2share(src).start()
 
     loop(1, 16, x2forward)
-    wbegin(wo2copy, 7, wo2, w2r)
+    wbegin(7, wo2, w2s, w2r)
 
     def mwait(s):
         src = lax.rem(lat + NLAT - s, NLAT)
@@ -432,6 +503,7 @@
         t2[h] = soft(k_aug, q_aug, v_aug)
 
     loop(0, 8, head2)
+    wpass(wo2, w2s, w2r, go, True)
     o2_s[...] = jnp.transpose(t2[...].reshape(384, 512)).astype(BF).reshape(2, 16, 16, 384)
 
     def bcopy(s):
@@ -466,14 +538,15 @@
     each_u1("finish")
     loop(0, 6, lambda k: u1share(k).wait_send())
 
-    @pl.when(sends)
-    def _():
-        loop(1, 16, lambda t: wo1copy(t).wait_send())
-        loop(1, 16, lambda t: wo2copy(t).wait_send())
+    wcast(3, wo1, w1s, w1r, left)
+    wpass(wo1, w1s, w1r, left, False)
+    wcast(7, wo2, w2s, w2r, left)
+    wpass(wo2, w2s, w2r, left, False)
 
     loop(0, 8, lambda k: wshare(wo1, w1r, w1f, k).wait_send())
     loop(0, 8, lambda k: wshare(wo2, w2r, w2f, k).wait_send())
-    u2do("finish")
+    u2do(left)
+    u2on(left)
     u2pass("finish")
 
     def osent(k):
@@ -524,8 +597,8 @@
             pltpu.VMEM((2, 16, 16, 384), BF),
             DMA((16,)), DMA((16,)), DMA, DMA, DMA((16,)), DMA((16,)), DMA((NLAT,)), DMA((2, 16)),
             DMA((4,)), DMA((4, 4)), DMA((4, 4)), DMA((3, 4)), DMA((12,)), DMA((6,)),
-            DMA((16,)), DMA((16,)), DMA((8,)), DMA((3, 16)), DMA((24,)), DMA((24,)),
-            DMA((16,)), DMA((16,)), DMA((8,)), DMA((4, 4)), DMA((16,)),
+            DMA((4, 4)), DMA((16,)), DMA((8,)), DMA((3, 4, 4)), DMA((24,)), DMA((24,)),
+            DMA((4, 4)), DMA((16,)), DMA((8,)), DMA((4, 4)), DMA((16,)),
             DMA((16,)), DMA((2, 16)), DMA((16,)), DMA((NLAT,)), DMA((2, 16)),
         ],
         compiler_params=pltpu.CompilerParams(

time: 139 us -> 125 us (0.90)
  the two profiles are of different devices: /device:TPU:31 before, /device:TPU:63 now
where the time goes in v4:
time: 125 us
  Pallas kernels  123 us (98%)
  local copies, waits for them, and re-layouts  1.77 us (1%)
    pallas_call x1, Pallas kernels, pair(): pl.pallas_call(pair_kernel, out_shape=jax.ShapeDtypeStruct((4, 64, D), BF...  123 us

profile of v4, /device:TPU:63, one launch (start us, length us, event | category | flops | bytes accessed | tf_op | source)
XLA Modules:
  0.0 124.9 jit_solution(12746009372658795023)
XLA Ops:
  0.0 123.2 %shard_map.100 = bf16[4,64,768]{2,1,0:T(8,128)(2,1)} custom-call(bf16[4,64,768]{2,1,0:T(8,128)(2,1)} %tok.1, s32[4,64]{1,0:T(4,128)} %sid.1, s32[4,64]{1,0:T(4,128)} %valid.1, f32[5,768]{1,0:T(8,128)} %table.1, f32[768]{0:T(1024)} %g1.1, f32[768]{0:T(1024)} %g2.1, bf16[24,144]{1,0:T(8,128)(2,1)} %wq1.1, bf16[24,48]{1,0:T(8,128)(2,1)} %wp1.1, ...), custom_call_target="tpu_custom_call" | custom-call | tf_op jit(solution)/shard_map/pallas_call | solution.py:566
  123.2 1.8 %copy.12 = bf16[4,64,768]{2,1,0:T(8,128)(2,1)} copy(bf16[4,64,768]{2,1,0:T(8,128)(2,1)} %shard_map.100) | data formatting | bytes 786432

commit v5 on v4

--- a/solution.py
+++ b/solution.py
@@ -171,11 +171,12 @@
         return remote(v1.at[to // 4], vl.at[lon], v1s.at[s], v1r.at[lon], lat, to)
 
     def v2copy(s):
-        to = lax.rem(lat + s, NLAT)
-        return remote(v2.at[to // 2], mv.at[core, place], v2s.at[s], v2r.at[core, place], to, lon)
+        to = lax.rem(place + s, 16)
+        return remote(
+            v2.at[to], mv.at[core, place], v2s.at[s], v2r.at[core, place], to * 2 + core, lon
+        )
 
     loop(1, 16, lambda s: v1copy(s).start())
-    loop(1, NLAT, lambda s: v2copy(s).start())
     vl[lon] = v1[a]
     mv[core, place] = v2[place]
 
@@ -383,6 +384,7 @@
         u1share(k).start()
 
     u2do(go)
+    loop(1, 16, lambda s: v2copy(s).start())
     loop(0, 6, u1forward)
     u2on(go)
     wbegin(3, wo1, w1s, w1r)
@@ -410,7 +412,9 @@
     def ocopy(bb, aa):
         return remote(o_s.at[bb, aa], land_o.at[lon], os.at[bb, aa], orr.at[lon], lat, aa * 4 + bb)
 
-    def block(qb):
+    def block(step):
+        qb = lax.rem(b + 1 + step, 4)
+
         def head(h):
             k_aug = jnp.concatenate([kv_s[h], ka1], axis=0)
             q_aug = jnp.concatenate([q_s[qb, h], qa1], axis=0)
@@ -422,20 +426,30 @@
         for aa in range(4):
             o_s[qb, aa, :, :192] = o[aa * 64 : (aa + 1) * 64]
 
-        def send(aa):
+        def send(k):
+            aa = lax.rem(a + 1 + k, 4)
+
             @pl.when(aa * 4 + qb != lon)
             def _():
                 ocopy(qb, aa).start()
 
         loop(0, 4, send)
-        u2pass("start", qb * 6, qb * 6 + 6)
-
-        @pl.when(qb == 1)
+        u2pass("start", step * 6, step * 6 + 6)
+
+        @pl.when(step == 1)
         def _():
             wpass(wo1, w1s, w1r, go, True)
 
 
     loop(0, 4, block)
+
+    def mwait(s):
+        src = lax.rem(place + 16 - s, 16)
+        arrived(mv.at[core, src], v2r.at[core, src]).wait()
+
+    loop(1, 16, mwait)
+    mshare = remote(mv.at[core], mv.at[core], v2s.at[0], v2r.at[core, 0], sib, lon)
+    mshare.start()
     land_o[lon] = o_s[b, a]
     wforward(wo1, w1r, w1f)
     loop(1, 16, lambda s: arrived(land_o.at[lax.rem(lon + s, 16)], orr.at[lax.rem(lon + s, 16)]).wait())
@@ -479,12 +493,7 @@
     loop(1, 16, x2forward)
     wbegin(7, wo2, w2s, w2r)
 
-    def mwait(s):
-        src = lax.rem(lat + NLAT - s, NLAT)
-        c, p = lax.rem(src, 2), src // 2
-        arrived(mv.at[c, p], v2r.at[c, p]).wait()
-
-    loop(1, NLAT, mwait)
+    arrived(mv.at[1 - core], v2r.at[1 - core, 0]).wait()
     loop(0, 24, u2rest)
     loop(0, 16, lambda k: arrived(col.at[1 - core, k], x2r.at[1 - core, k]).wait())
 
@@ -532,7 +541,8 @@
     loop(1, 16, lambda s: wcopy(s).wait_send())
     sibling.wait_send()
     loop(1, 16, lambda s: v1copy(s).wait_send())
-    loop(1, NLAT, lambda s: v2copy(s).wait_send())
+    loop(1, 16, lambda s: v2copy(s).wait_send())
+    mshare.wait_send()
     loop(1, 4, lambda s: ycopy(s).wait_send())
     loop(1, 4, lambda s: loop(0, 4, lambda aa: xcopy(s, aa).wait_send()))
     each_u1("finish")

time: 125 us -> 121 us (0.968)
  the two profiles are of different devices: /device:TPU:63 before, /device:TPU:1 now
where the time goes in v5:
time: 121 us; the launch traced here: 119 us
  Pallas kernels  118 us (98%)
  local copies, waits for them, and re-layouts  1.77 us (1%)
    pallas_call x1, Pallas kernels, pair(): pl.pallas_call(pair_kernel, out_shape=jax.ShapeDtypeStruct((4, 64, D), BF...  118 us

profile of v5, /device:TPU:1, one launch (start us, length us, event | category | flops | bytes accessed | tf_op | source)
XLA Modules:
  0.0 119.4 jit_solution(341127394197981050)
XLA Ops:
  0.0 117.7 %shard_map.100 = bf16[4,64,768]{2,1,0:T(8,128)(2,1)} custom-call(bf16[4,64,768]{2,1,0:T(8,128)(2,1)} %tok.1, s32[4,64]{1,0:T(4,128)} %sid.1, s32[4,64]{1,0:T(4,128)} %valid.1, f32[5,768]{1,0:T(8,128)} %table.1, f32[768]{0:T(1024)} %g1.1, f32[768]{0:T(1024)} %g2.1, bf16[24,144]{1,0:T(8,128)(2,1)} %wq1.1, bf16[24,48]{1,0:T(8,128)(2,1)} %wp1.1, ...), custom_call_target="tpu_custom_call" | custom-call | tf_op jit(solution)/shard_map/pallas_call | solution.py:576
  117.7 1.8 %copy.12 = bf16[4,64,768]{2,1,0:T(8,128)(2,1)} copy(bf16[4,64,768]{2,1,0:T(8,128)(2,1)} %shard_map.100) | data formatting | bytes 786432

commit v6 on v5

--- a/solution.py
+++ b/solution.py
@@ -176,7 +176,6 @@
             v2.at[to], mv.at[core, place], v2s.at[s], v2r.at[core, place], to * 2 + core, lon
         )
 
-    loop(1, 16, lambda s: v1copy(s).start())
     vl[lon] = v1[a]
     mv[core, place] = v2[place]
 
@@ -228,6 +227,7 @@
                 loop(0, 4, dest)
 
     each_u1("start")
+    loop(1, 16, lambda s: v1copy(s).start())
 
     sends = lax.rem(b, 2) == core
 

time: 121 us -> 121 us (level)
  no operation moved by 1% of the time
where the time goes in v6:
time: 121 us; the launch traced here: 120 us
  Pallas kernels  118 us (98%)
  local copies, waits for them, and re-layouts  1.77 us (1%)
    pallas_call x1, Pallas kernels, pair(): pl.pallas_call(pair_kernel, out_shape=jax.ShapeDtypeStruct((4, 64, D), BF...  118 us

profile of v6, /device:TPU:1, one launch (start us, length us, event | category | flops | bytes accessed | tf_op | source)
XLA Modules:
  0.0 119.9 jit_solution(13829254634993375663)
XLA Ops:
  0.0 118.2 %shard_map.100 = bf16[4,64,768]{2,1,0:T(8,128)(2,1)} custom-call(bf16[4,64,768]{2,1,0:T(8,128)(2,1)} %tok.1, s32[4,64]{1,0:T(4,128)} %sid.1, s32[4,64]{1,0:T(4,128)} %valid.1, f32[5,768]{1,0:T(8,128)} %table.1, f32[768]{0:T(1024)} %g1.1, f32[768]{0:T(1024)} %g2.1, bf16[24,144]{1,0:T(8,128)(2,1)} %wq1.1, bf16[24,48]{1,0:T(8,128)(2,1)} %wp1.1, ...), custom_call_target="tpu_custom_call" | custom-call | tf_op jit(solution)/shard_map/pallas_call | solution.py:576
  118.2 1.8 %copy.12 = bf16[4,64,768]{2,1,0:T(8,128)(2,1)} copy(bf16[4,64,768]{2,1,0:T(8,128)(2,1)} %shard_map.100) | data formatting | bytes 786432
